TPU v7x, 32 devices: a whole 2x2x4 slice. The times are simulated.
32 devices in a mesh: sec: 2 (over y), seq: 4 (over x, core), trk: 4 (over z).
Axes of the slice: x: 2, y: 2, z: 4, core: 2. Of those that a mesh axis runs over, the one named last changes fastest.
Arguments:
- tokens: bfloat16 [8, 256, 1536], P('sec', 'seq'), may hold values from -6 to 6
- norm_gain: bfloat16 [1536], replicated, may hold values from 0.25 to 1.75
- dilated_conv_weight: bfloat16 [1536, 3, 1536], P(None, None, 'trk'), may hold values from -0.09375 to 0.09375
- head_weight: bfloat16 [1536, 4, 40, 128], P(None, 'trk'), may hold values from -0.15625 to 0.15625
- targets: bfloat16 [8, 256, 4, 40, 128], P('sec', 'seq', 'trk'), may hold values from 0 to 2
- owner_tiles: int32 [4, 40], P('trk'), may hold values from -1 to 80, as said below
- species: int32 [8], P('sec'), may hold values from 0 to 1, as said below
Outputs:
- conv_grad: float32 [1536, 3, 1536], P(('sec', 'seq'), None, 'trk')
- head_grad: float32 [1536, 4, 40, 128], P(('sec', 'seq'), 'trk')
Inputs may be any that keep to these rules, and one draw needn't show every extreme that they name: `owner_tiles`: each of the 81 tiles (human tiles 0 to 59, then the mouse tiles) stands in exactly one slot of one owner; -1 marks an empty slot; in every draw one owner has all 40 slots filled. `species`: 0 is human, 1 is mouse; exactly half of the samples are mouse.
All inputs are finite; a program needn't handle non-finite values.
Results may differ from a plain program's by a relative error of at most 0.0023.
Values may be sent and summed in bfloat16 or wider, within the bound.
A program may use at most 192 MiB of HBM per device.

v0:
```python
import math

import jax
import jax.numpy as jnp
from jax import lax
from jax.sharding import PartitionSpec as P

HTRACKS = 7611
MTRACKS = 2608
DILATION_BINS = 16
HTILES = 60


grad_clip = 0.1


def padded(cells, sides, width):
    for axis, dim in sides:
        count = lax.axis_size(axis)
        ends = count - 1
        head = lax.slice_in_dim(cells, 0, width, axis=dim)
        tail = lax.slice_in_dim(cells, cells.shape[dim] - width, cells.shape[dim], axis=dim)
        cells = jnp.concatenate(
            [
                lax.ppermute(tail, axis, [(i, (i + 1) % count) for i in range(ends)]),
                cells,
                lax.ppermute(head, axis, [((i + 1) % count, i) for i in range(ends)]),
            ],
            axis=dim,
        )
    return cells


def contracted_rows(left, right):
    return lax.dot_general(
        left, right, (((0,), (0,)), ((), ())), preferred_element_type=jnp.float32
    )


def body(tokens, norm_gain, dilated_conv_weight, head_weight, targets, owner_tiles, species):
    sample_count = tokens.shape[0]
    local_rows = tokens.shape[1]
    width_all = tokens.shape[2]
    tap_count = dilated_conv_weight.shape[1]
    out_share = dilated_conv_weight.shape[2]
    slot_count = head_weight.shape[2]
    lane_count = head_weight.shape[3]
    inputs = tokens.astype(jnp.float32)
    mean_sq = jnp.mean(inputs * inputs, axis=-1, keepdims=True)
    normed = inputs * lax.rsqrt(mean_sq + 1e-06) * norm_gain.astype(jnp.float32)
    hidden_state = jax.nn.gelu(normed).astype(jnp.bfloat16)
    padded_input = padded(hidden_state, (("seq", 1),), DILATION_BINS)
    convolution_output = jnp.zeros((sample_count, local_rows, out_share), jnp.float32)
    for kernel_tap_index in range(tap_count):
        convolution_output = convolution_output + jnp.dot(
            padded_input[
                :, kernel_tap_index * DILATION_BINS : kernel_tap_index * DILATION_BINS + local_rows
            ],
            dilated_conv_weight[:, kernel_tap_index, :],
            preferred_element_type=jnp.float32,
        )
    own_cols = lax.dynamic_slice_in_dim(inputs, lax.axis_index("trk") * out_share, out_share, 2)
    mixed_share = (own_cols + convolution_output).astype(jnp.bfloat16)
    mixed_all = lax.all_gather(mixed_share, "trk", axis=2, tiled=True)
    tiles_here = owner_tiles[0]
    is_mouse = tiles_here >= HTILES
    within = jnp.where(is_mouse, tiles_here - HTILES, tiles_here)
    track_limit = jnp.where(is_mouse, MTRACKS, HTRACKS).astype(jnp.int32)
    lane_ids = jnp.arange(lane_count, dtype=jnp.int32)
    lane_mask = (within[:, None] * lane_count + lane_ids[None, :] < track_limit[:, None]).astype(
        jnp.float32
    )
    grad_scale = 1.0 / math.sqrt(
        lax.axis_size("sec") * sample_count * lax.axis_size("seq") * local_rows
    )
    weights_here = head_weight[:, 0]
    delta_list = []
    back_list = []
    for sample_input in range(sample_count):
        active_int = ((tiles_here >= 0) & (is_mouse == (species[sample_input] == 1))).astype(
            jnp.int32
        )
        slot_order = jnp.argsort(1 - active_int, stable=True)
        live_count = jnp.sum(active_int)
        mixed_here = mixed_all[sample_input]
        target_here = targets[sample_input, :, 0]

        def slot_step(position, loop_state):
            deltas, back_sum = loop_state
            slot_index = slot_order[position]
            column_w = lax.dynamic_index_in_dim(weights_here, slot_index, 1, keepdims=False)
            logits = jnp.dot(mixed_here, column_w, preferred_element_type=jnp.float32)
            target_cols = lax.dynamic_index_in_dim(
                target_here, slot_index, 1, keepdims=False
            ).astype(jnp.float32)
            mask_row = lax.dynamic_index_in_dim(lane_mask, slot_index, 0, keepdims=False)
            delta_f = (
                grad_scale
                * (jax.nn.softplus(logits) - target_cols)
                * jax.nn.sigmoid(logits)
                * mask_row[None, :]
            )
            delta_b = delta_f.astype(jnp.bfloat16)
            deltas = lax.dynamic_update_index_in_dim(deltas, delta_b, slot_index, 1)
            back_sum = back_sum + lax.dot_general(
                delta_b, column_w, (((1,), (1,)), ((), ())), preferred_element_type=jnp.float32
            )
            return (deltas, back_sum)

        start_state = (
            jnp.zeros((local_rows, slot_count, lane_count), jnp.bfloat16),
            jnp.zeros((local_rows, width_all), jnp.float32),
        )
        deltas_one, back_one = lax.fori_loop(0, live_count, slot_step, start_state)
        delta_list.append(deltas_one)
        back_list.append(back_one)
    deltas = jnp.stack(delta_list)
    back_sum = jnp.stack(back_list)
    backward_portion = lax.psum_scatter(back_sum, "trk", scatter_dimension=2, tiled=True).astype(
        jnp.bfloat16
    )
    group_count = lax.axis_size("sec") * lax.axis_size("seq")
    share_rows = width_all // group_count
    per_tap = [
        lax.dot_general(
            padded_input[
                :, kernel_tap_index * DILATION_BINS : kernel_tap_index * DILATION_BINS + local_rows
            ],
            backward_portion,
            (((0, 1), (0, 1)), ((), ())),
            preferred_element_type=jnp.float32,
        )
        for kernel_tap_index in range(tap_count)
    ]
    conv_grad = lax.psum_scatter(
        jnp.stack(per_tap, axis=1), ("sec", "seq"), scatter_dimension=0, tiled=True
    )
    flat_mixed = mixed_all.reshape(sample_count * local_rows, width_all)
    flat_deltas = deltas.reshape(sample_count * local_rows, slot_count * lane_count)
    whole_sum = lax.psum(contracted_rows(flat_mixed, flat_deltas), ("sec", "seq"))
    total_sq = lax.psum(jnp.sum(whole_sum * whole_sum), "trk")
    grad_share = lax.dynamic_slice_in_dim(
        whole_sum, lax.axis_index(("sec", "seq")) * share_rows, share_rows, 0
    )
    entries = width_all * lax.axis_size("trk") * slot_count * lane_count
    factor = jnp.minimum(1.0, grad_clip * lax.rsqrt(total_sq / entries + 1e-06))
    head_grad = (grad_share * factor).reshape(share_rows, 1, slot_count, lane_count)
    return (conv_grad, head_grad)


def solution(mesh):
    return jax.shard_map(
        body,
        mesh=mesh,
        in_specs=(
            P("sec", "seq", None),
            P(),
            P(None, None, "trk"),
            P(None, "trk", None, None),
            P("sec", "seq", "trk", None, None),
            P("trk", None),
            P("sec"),
        ),
        out_specs=(P(("sec", "seq"), None, "trk"), P(("sec", "seq"), "trk", None, None)),
        check_vma=False,
    )
```

profile of v0, /device:TPU:0, one launch (start us, length us, event | category | flops | bytes accessed | tf_op | source)
XLA Modules:
  0.0 1034.5 jit_solution(15960789532844439914)
XLA Ops:
  12.7 2.4 collective-permute-start
  21.0 2.6 fusion.71
  24.9 14.5 %copy.36 = bf16[1536,1,40,128]{3,0,2,1:T(8,128)(2,1)} copy(bf16[1536,1,40,128]{3,2,1,0:T(8,128)(2,1)} %param.18) | data formatting | bytes 31457280 | tf_op args[3]
  40.2 2.1 sort.59
  42.3 2.1 sort.60
  44.4 2.1 sort.61
  46.5 2.1 sort.62
  48.6 2.6 copy_bitcast_fusion.3
  54.8 19.6 %all_gather.3 = bf16[4,64,1536]{2,1,0:T(8,128)(2,1)S(1)} all-gather(bf16[4,64,384]{2,1,0:T(8,128)(2,1)S(1)} %fusion.77), channel_id=1, replica_groups=mesh['sec'=2,'seq'=4,'trk'=4] {'trk'}, dimensions={2}, use_global_device_ids=true | all-gather | bytes 983040 | tf_op jit(solution)/shard_map/all_gather | solution.py:64
  75.4 42.4 %while.51 = (s32[]{:T(128)}, bf16[64,40,128]{2,0,1:T(8,128)(2,1)S(1)}, f32[64,1536]{1,0:T(8,128)S(1)}, s32[]{:T(128)}, s32[40]{0:T(128)S(1)}, /*index=5*/bf16[15...) while((s32[]{:T(128)}, ...), condition=%wide.region_16.17_spmd, body=%wide.region_15.16_spmd.sunk | while | flops 50552840 | bytes 1837781 | solution.py:114
  118.9 41.0 %while.50 = (s32[]{:T(128)}, bf16[64,40,128]{2,0,1:T(8,128)(2,1)S(1)}, f32[64,1536]{1,0:T(8,128)S(1)}, s32[]{:T(128)}, s32[40]{0:T(128)S(1)}, /*index=5*/bf16[15...) while((s32[]{:T(128)}, ...), condition=%wide.region_12.13_spmd, body=%wide.region_11.12_spmd.sunk | while | flops 50552840 | bytes 1837781 | solution.py:114
  161.0 64.7 %while.49 = (s32[]{:T(128)}, bf16[64,40,128]{2,0,1:T(8,128)(2,1)S(1)}, f32[64,1536]{1,0:T(8,128)S(1)}, s32[]{:T(128)}, s32[40]{0:T(128)S(1)}, /*index=5*/bf16[15...) while((s32[]{:T(128)}, ...), condition=%wide.region_8.9_spmd, body=%wide.region_7.8_spmd.sunk | while | flops 50552840 | bytes 1837781 | solution.py:114
  227.5 70.7 %while.48 = (s32[]{:T(128)}, bf16[64,40,128]{2,0,1:T(8,128)(2,1)}, f32[64,1536]{1,0:T(8,128)S(1)}, s32[]{:T(128)}, s32[40]{0:T(128)S(1)}, /*index=5*/bf16[1536,4...) while((s32[]{:T(128)}, bf16[64,40,128]{2,0,1:T(8,128)(2,1)}, ...), condition=%wide.region_4.5_spmd, body=%wide.region_3.4_spmd.sunk | while | flops 50552840 | bytes 1837781 | solution.py:114
  237.1 1.9 bitcast_dynamic-update-slice_fusion.8
  299.8 2.0 pad_maximum_fusion.1
  303.6 12.4 %fusion.56 = f32[1536,5120]{1,0:T(8,128)} fusion(bf16[256,1536]{1,0:T(8,128)(2,1)S(1)} %bitcast.264, bf16[32,8,40,128]{3,2,1,0:T(8,128)(2,1)S(1)} %bitcast.263), kind=kOutput, calls=%fused_computation.75 | convolution fusion | flops 4026531840 | bytes 34865152 | tf_op jit(solution)/shard_map/dot_general | solution.py:35
  316.1 285.1 %reduce-scatter.3.cloned.1.call-done = f32[4,64,384]{2,1,0:T(8,128)} async-done(((f32[4,64,1536]{2,1,0:T(8,128)}), f32[4,64,384]{2,1,0:T(8,128)}) %reduce-scatter.3.cloned.1.call-update) | async-done | bytes 393232 | tf_op jit(solution)/shard_map/reduce_scatter | solution.py:119
  604.0 3.3 pad_maximum_fusion
  607.4 349.8 %all-reduce.2.cloned.1.call-done = f32[1536,5120]{1,0:T(8,128)} async-done(((f32[1536,5120]{1,0:T(8,128)}), f32[1536,5120]{1,0:T(8,128)}) %all-reduce.2.cloned.1.call-update) | async-done | bytes 31457296 | tf_op jit(solution)/shard_map/psum | solution.py:140
  957.2 15.5 %multiply_reduce_fusion = f32[]{:T(128)} fusion(f32[1536,5120]{1,0:T(8,128)} %all-reduce.2.cloned.1.call-done), kind=kLoop, calls=%fused_computation.68 | loop fusion | flops 15728639 | bytes 31457284 | tf_op jit(solution)/shard_map/reduce_sum | solution.py:141
  972.8 12.4 %psum.15 = f32[]{:T(128)} all-reduce(f32[]{:T(128)} %multiply_reduce_fusion), channel_id=1, replica_groups=mesh['sec'=2,'seq'=4,'trk'=4] {'trk'}, use_global_device_ids=true, to_apply=%region_21.22 | all-reduce | flops 1 | bytes 8 | tf_op jit(solution)/shard_map/psum | solution.py:141
  985.8 3.1 multiply_bitcast_fusion
  989.0 2.6 copy.26
  991.6 35.5 %reduce-scatter.5.cloned.1.call-done = f32[192,3,384]{2,0,1:T(8,128)} async-done(((f32[1536,3,384]{2,0,1:T(8,128)}), f32[192,3,384]{2,0,1:T(8,128)}) %reduce-scatter.5.cloned.1.call-update) | async-done | bytes 884752 | tf_op jit(solution)/shard_map/reduce_scatter | solution.py:135
  (211 shorter events, 144.1 us)
Async XLA Ops:
  8.0 8.4 copy-start
  8.0 9.8 copy-start.10
  8.0 593.1 %reduce-scatter.3.cloned.1.call-start = ((), (), s32[]{:S(2)}) async-start(), calls=%async_computation.2 | async-start | bytes 1966080 | tf_op jit(solution)/shard_map/reduce_scatter | solution.py:119
  12.7 40.4 %collective-permute-start = (bf16[4,16,1536]{2,1,0:T(8,128)(2,1)S(1)}, bf16[4,16,1536]{2,1,0:T(8,128)(2,1)S(1)}, u32[]{:S(2)}, u32[]{:S(2)}) collective-permute-start(bf16[4,16,1536]{2,1,0:T(8,128)(2,1)S(1)} %get-tuple-element.310), channel_id=1, source_target_pairs={{0,4},{4,8},{8,12},{1,5},{5,9},{9,13},{2,6},{6,10},{10,14},{3,7},{... | collective-permute-start | bytes 589832 | tf_op jit(solution)/shard_map/ppermute | solution.py:25
  15.1 37.4 %collective-permute-start.1 = (bf16[4,16,1536]{2,1,0:T(8,128)(2,1)}, bf16[4,16,1536]{2,1,0:T(8,128)(2,1)S(1)}, u32[]{:S(2)}, u32[]{:S(2)}) collective-permute-start(bf16[4,16,1536]{2,1,0:T(8,128)(2,1)} %get-tuple-element.311), channel_id=1, source_target_pairs={{4,0},{8,4},{12,8},{5,1},{9,5},{13,9},{6,2},{10,6},{14,10},{7,3},{... | collective-permute-start | bytes 589832 | tf_op jit(solution)/shard_map/ppermute | solution.py:27
  17.8 5.9 copy-start.5
  24.9 14.5 %copy-start.11 = (s32[1,40]{1,0:T(1,128)S(1)}, s32[1,40]{1,0:T(1,128)}, u32[]{:S(2)}) copy-start(s32[1,40]{1,0:T(1,128)} %param.20) | copy-start | bytes 484
  48.6 3.9 copy-start.12
  51.2 1.9 copy-start.13
  52.5 2.3 copy-start.8
  53.1 22.1 %copy-start.6 = (bf16[4,16,1536]{2,1,0:T(8,128)(2,1)}, bf16[4,16,1536]{2,1,0:T(8,128)(2,1)S(1)}, u32[]{:S(2)}) copy-start(bf16[4,16,1536]{2,1,0:T(8,128)(2,1)S(1)} %collective-permute-done) | copy-start | bytes 589828
  117.9 0.8 copy-start.2
  159.9 0.9 copy-start.3
  225.7 0.9 copy-start.4
  299.6 657.6 %all-reduce.2.cloned.1.call-start = ((), (), s32[]{:S(2)}) async-start(), calls=%async_computation.4 | async-start | bytes 62914560 | tf_op jit(solution)/shard_map/psum | solution.py:140
  316.0 285.2 %copy-start.9 = (bf16[4,16,1536]{2,1,0:T(8,128)(2,1)S(1)}, bf16[4,16,1536]{2,1,0:T(8,128)(2,1)}, u32[]{:S(2)}) copy-start(bf16[4,16,1536]{2,1,0:T(8,128)(2,1)} %copy-done.8) | copy-start | bytes 589828
  316.0 286.8 %copy-start.7 = (bf16[4,16,1536]{2,1,0:T(8,128)(2,1)S(1)}, bf16[4,16,1536]{2,1,0:T(8,128)(2,1)}, u32[]{:S(2)}) copy-start(bf16[4,16,1536]{2,1,0:T(8,128)(2,1)} %copy-done.6) | copy-start | bytes 589828
  316.0 711.1 %reduce-scatter.5.cloned.1.call-start = ((), (), s32[]{:S(2)}) async-start(), calls=%async_computation.3 | async-start | bytes 7962624 | tf_op jit(solution)/shard_map/reduce_scatter | solution.py:135
  601.2 1.7 copy-start.1
Sparse Core Ops, SparseCore 0:
  299.7 301.3 reduce-scatter.2
Sparse Core Ops, SparseCore 1:
  316.1 641.1 all-reduce.1
  961.6 65.4 reduce-scatter.4
where the time goes:
time: 1040 us; the launch traced here: 1030 us
  waiting for transfers between devices  670 us (64%)
  matrix products  119 us (11%)
  loops' own time  97.5 us (9%)
  local copies, waits for them, and re-layouts  53 us (5%)
  other arithmetic  39.8 us (4%)
  blocking collectives  32 us (3%)
  between operations  19.1 us (2%)
    psum x1, waiting for transfers between devices, body(): lax.psum(contracted_rows(flat_mixed, flat_deltas), ('sec', 'seq'))  350 us
    reduce_scatter x1, waiting for transfers between devices, body(): lax.psum_scatter(back_sum, 'trk', scatter_dimension=2, tiled=True)  285 us
    another operation x4, loops' own time, body(): deltas_one, back_one = lax.fori_loop(0, live_count, slot_step, start_state)  97.5 us
    dot_general x36, matrix products, slot_step(): logits = jnp.dot(mixed_here, column_w, preferred_element_type=jnp.float32)  53.2 us
    dot_general x36, matrix products, slot_step(): lax.dot_general(delta_b, column_w, (((1,), (1,)), ((), ())), preferred_el...  45.4 us
    reduce_scatter x1, waiting for transfers between devices, body(): lax.psum_scatter(jnp.stack(per_tap, axis=1), ('sec', 'seq'), scatter_dime...  35.5 us
    dynamic_slice x36, local copies, waits for them, and re-layouts, slot_step(): slot_index = slot_order[position]  22.5 us
  transfers between devices with their start and end apart: 5, of which 3 were waited for; matrix products, arithmetic and copies ran while one was open for 7% of the time, Pallas kernels for 0%

commit v1 on v0

v1 whole, which is shorter than its diff:
```python
import math

import jax
import jax.numpy as jnp
from jax import lax
from jax.sharding import PartitionSpec as P

HTRACKS = 7611
MTRACKS = 2608
DILATION_BINS = 16
HTILES = 60
GRAD_CLIP = 0.1
SEND = jnp.float32


def padded(cells, axis, dim, width):
    count = lax.axis_size(axis)
    ends = count - 1
    head = lax.slice_in_dim(cells, 0, width, axis=dim)
    tail = lax.slice_in_dim(cells, cells.shape[dim] - width, cells.shape[dim], axis=dim)
    return jnp.concatenate(
        [
            lax.ppermute(tail, axis, [(i, (i + 1) % count) for i in range(ends)]),
            cells,
            lax.ppermute(head, axis, [((i + 1) % count, i) for i in range(ends)]),
        ],
        axis=dim,
    )


def live_mask(owner_tiles, species, lane_count):
    tiles = owner_tiles[0]
    is_mouse = tiles >= HTILES
    within = jnp.where(is_mouse, tiles - HTILES, tiles)
    limit = jnp.where(is_mouse, MTRACKS, HTRACKS).astype(jnp.int32)
    lanes = jnp.arange(lane_count, dtype=jnp.int32)
    valid = (within[:, None] * lane_count + lanes[None, :] < limit[:, None]) & (tiles >= 0)[:, None]
    live = is_mouse[None, :] == (species == 1)[:, None]
    return (live[:, :, None] & valid[None]).astype(jnp.float32)


def body(tokens, norm_gain, dilated_conv_weight, head_weight, targets, owner_tiles, species):
    samples, bins, width = tokens.shape
    taps = dilated_conv_weight.shape[1]
    out_share = dilated_conv_weight.shape[2]
    slots, lanes = head_weight.shape[2:]
    owners = lax.axis_size("trk")
    rows = samples * bins
    columns = slots * lanes

    inputs = tokens.astype(jnp.float32)
    mean_sq = jnp.mean(inputs * inputs, axis=-1, keepdims=True)
    normed = inputs * lax.rsqrt(mean_sq + 1e-06) * norm_gain.astype(jnp.float32)
    hidden = jax.nn.gelu(normed).astype(jnp.bfloat16)
    hidden = padded(hidden, "seq", 1, DILATION_BINS)
    shifted = [
        hidden[:, k * DILATION_BINS : k * DILATION_BINS + bins].reshape(rows, width)
        for k in range(taps)
    ]
    conv = sum(
        jnp.dot(shifted[k], dilated_conv_weight[:, k, :], preferred_element_type=jnp.float32)
        for k in range(taps)
    )
    own = lax.dynamic_slice_in_dim(tokens, lax.axis_index("trk") * out_share, out_share, 2)
    mixed_share = (own.reshape(rows, out_share).astype(jnp.float32) + conv).astype(jnp.bfloat16)
    gathered = lax.all_gather(mixed_share, "trk", axis=0)
    mixed = jnp.concatenate([gathered[g] for g in range(owners)], axis=-1)

    weights = head_weight.reshape(width, columns)
    mask = live_mask(owner_tiles, species, lanes).reshape(samples, 1, columns)
    grad_scale = 1.0 / math.sqrt(
        lax.axis_size("sec") * samples * lax.axis_size("seq") * bins
    )
    logits = jnp.dot(mixed, weights, preferred_element_type=jnp.float32)
    decay = jnp.exp(-jnp.abs(logits))
    softplus = jnp.maximum(logits, 0.0) + jnp.log(1.0 + decay)
    sigmoid = jnp.where(logits >= 0, 1.0, decay) / (1.0 + decay)
    wanted = targets.reshape(rows, columns).astype(jnp.float32)
    spread = jnp.broadcast_to(mask * grad_scale, (samples, bins, columns)).reshape(rows, columns)
    delta = (spread * (softplus - wanted) * sigmoid).astype(jnp.bfloat16)

    raw = lax.dot_general(
        mixed, delta, (((0,), (0,)), ((), ())), preferred_element_type=jnp.float32
    ).astype(SEND)
    raw = lax.psum_scatter(raw, ("sec", "seq"), scatter_dimension=0, tiled=True)
    raw = raw.astype(jnp.float32)

    back = lax.dot_general(
        delta, weights, (((1,), (1,)), ((), ())), preferred_element_type=jnp.float32
    )
    back = jnp.stack([back[:, g * out_share : (g + 1) * out_share] for g in range(owners)])
    back = lax.psum_scatter(back, "trk", scatter_dimension=0, tiled=True)[0].astype(jnp.bfloat16)
    conv_part = jnp.concatenate(
        [
            lax.dot_general(
                shifted[k], back, (((0,), (0,)), ((), ())), preferred_element_type=jnp.float32
            )
            for k in range(taps)
        ],
        axis=1,
    ).astype(SEND)
    conv_grad = lax.psum_scatter(conv_part, ("sec", "seq"), scatter_dimension=0, tiled=True)
    conv_grad = conv_grad.astype(jnp.float32).reshape(-1, taps, out_share)

    total_sq = lax.psum(jnp.sum(raw * raw), ("sec", "seq", "trk"))
    entries = width * owners * columns
    factor = jnp.minimum(1.0, GRAD_CLIP * lax.rsqrt(total_sq / entries + 1e-06))
    head_grad = (raw * factor).reshape(-1, 1, slots, lanes)
    return conv_grad, head_grad


def solution(mesh):
    return jax.shard_map(
        body,
        mesh=mesh,
        in_specs=(
            P("sec", "seq", None),
            P(),
            P(None, None, "trk"),
            P(None, "trk", None, None),
            P("sec", "seq", "trk", None, None),
            P("trk", None),
            P("sec"),
        ),
        out_specs=(P(("sec", "seq"), None, "trk"), P(("sec", "seq"), "trk", None, None)),
        check_vma=False,
    )
```

time: 1040 us -> 442 us (0.42)
  waiting for transfers between devices: 670 us -> 277 us
  loops' own time: 97.5 us -> 0 us
  matrix products: 119 us -> 47.2 us
  local copies, waits for them, and re-layouts: 53 us -> 17.4 us
  blocking collectives: 32 us -> 59.9 us
  other arithmetic: 39.8 us -> 20.1 us
    psum x1 -> x0, waiting for transfers between devices: 350 us -> none  [body(): lax.psum(contracted_rows(flat_mixed, flat_deltas), ('sec', 'seq'))]
    another operation x4 -> x0, loops' own time: 97.5 us -> none  [body(): deltas_one, back_one = lax.fori_loop(0, live_count, slot_step, start_state)]
    reduce_scatter x2, waiting for transfers between devices: 321 us -> 230 us  [the longest x1 192 us: body(): raw = lax.psum_scatter(raw, ('sec', 'seq'), scatter_dimension=0, tiled=True)]
    dot_general x79 -> x9, matrix products: 119 us -> 47.2 us  [the longest x1 15.9 us: body(): lax.dot_general(mixed, delta, (((0,), (0,)), ((), ())), preferred_element...]
    unnamed x3 -> x4, waiting for transfers between devices: 0.05 us -> 47.8 us
    psum x1, blocking collectives: 12.4 us -> 39.5 us  [body(): total_sq = lax.psum(jnp.sum(raw * raw), ('sec', 'seq', 'trk'))]
    dynamic_slice x36 -> x1, local copies, waits for them, and re-layouts: 22.5 us -> 1.1 us  [body(): lax.dynamic_slice_in_dim(tokens, lax.axis_index('trk') * out_share, out_s...]
    reduce_sum x1, other arithmetic: 15.5 us -> 3.73 us  [body(): total_sq = lax.psum(jnp.sum(raw * raw), ('sec', 'seq', 'trk'))]
  transfers between devices with their start and end apart: 5 -> 5, of which waited for: 3 -> 3; matrix products, arithmetic and copies ran while one was open for 7% -> 6% of each run, Pallas kernels for 0% -> 0%
where the time goes in v1:
time: 442 us; the launch traced here: 441 us
  waiting for transfers between devices  277 us (63%)
  blocking collectives  59.9 us (14%)
  matrix products  47.2 us (11%)
  other arithmetic  20.1 us (5%)
  local copies, waits for them, and re-layouts  17.4 us (4%)
  between operations  14.7 us (3%)
  starting transfers between devices  4.64 us (1%)
    reduce_scatter x1, waiting for transfers between devices, body(): raw = lax.psum_scatter(raw, ('sec', 'seq'), scatter_dimension=0, tiled=True)  192 us
    unnamed x4, waiting for transfers between devices  47.8 us
    psum x1, blocking collectives, body(): total_sq = lax.psum(jnp.sum(raw * raw), ('sec', 'seq', 'trk'))  39.5 us
    reduce_scatter x1, waiting for transfers between devices, body(): lax.psum_scatter(back, 'trk', scatter_dimension=0, tiled=True)[0]  37.3 us
    all_gather x1, blocking collectives, body(): gathered = lax.all_gather(mixed_share, 'trk', axis=0)  20.4 us
    dot_general x1, matrix products, body(): lax.dot_general(mixed, delta, (((0,), (0,)), ((), ())), preferred_element...  15.9 us
    unnamed x31, local copies, waits for them, and re-layouts  14.3 us
    dot_general x1, matrix products, body(): logits = jnp.dot(mixed, weights, preferred_element_type=jnp.float32)  12.6 us
  transfers between devices with their start and end apart: 5, of which 3 were waited for; matrix products, arithmetic and copies ran while one was open for 6% of the time, Pallas kernels for 0%

profile of v1, /device:TPU:0, one launch (start us, length us, event | category | flops | bytes accessed | tf_op | source)
XLA Modules:
  0.0 441.4 jit_solution(2325461166506419737)
XLA Ops:
  7.2 1.4 fusion.11
  9.3 2.0 fusion.15
  12.2 3.0 collective-permute-start
  17.7 2.6 fusion.25
  20.3 2.9 convert.4
  24.4 1.4 pad_maximum_fusion.3
  25.8 2.4 fusion.23
  28.3 1.9 fusion.31
  30.2 20.4 %all-gather = bf16[1024,384]{1,0:T(8,128)(2,1)S(1)} all-gather(bf16[256,384]{1,0:T(8,128)(2,1)S(1)} %fusion.31), channel_id=2, replica_groups=mesh['sec'=2,'seq'=4,'trk'=4] {'trk'}, dimensions={0}, use_global_device_ids=true | all-gather | bytes 983040 | tf_op jit(solution)/shard_map/all_gather | solution.py:66
  51.4 12.6 %fusion.8 = bf16[256,5120]{1,0:T(8,128)(2,1)S(1)} fusion(f32[32,8,40,128]{3,2,1,0:T(8,128)S(1)} %bitcast.93, f32[4,5120]{1,0:T(4,128)} %fusion.41, bf16[192,8,40,128]{3,2,1,0:T(8,128)(2,1)} %bitcast.94, bf16[256,384]{1,0:T(8,128)(2,1)} %get-tuple-element.15, bf16[256,384]{1,0:T(8,128)(2,1)S(1)} %get-tuple-element.13, ...), kind=kOutput, calls=%fused_computation.10 | convolution fusion | flops 4045406208 | bytes 24461312 | tf_op jit(solution)/shard_map/dot_general | solution.py:74
  64.0 7.8 %fusion = f32[256,1536]{1,0:T(8,128)S(1)} fusion(bf16[256,5120]{1,0:T(8,128)(2,1)S(1)} %fusion.8, bf16[192,8,40,128]{3,2,1,0:T(8,128)(2,1)} %bitcast.95), kind=kOutput, calls=%fused_computation | convolution fusion | flops 4026531840 | bytes 19922944 | tf_op jit(solution)/shard_map/dot_general | solution.py:88
  73.3 37.3 %reduce-scatter.6.cloned.1.call-done = f32[1,256,384]{2,1,0:T(8,128)} async-done(((f32[4,256,384]{2,1,0:T(8,128)}), f32[1,256,384]{2,1,0:T(8,128)}) %reduce-scatter.6.cloned.1.call-update) | async-done | bytes 393232 | tf_op jit(solution)/shard_map/reduce_scatter | solution.py:92
  110.5 1.8 fusion.34
  112.3 1.7 fusion.36
  114.6 3.3 pad_maximum_fusion
  117.8 8.0 %copy.15 = f32[1536,1152]{1,0:T(8,128)} copy(f32[1536,1152]{0,1:T(8,128)} %pad_maximum_fusion) | data formatting | bytes 14155776
  126.9 15.9 %fusion.40 = f32[1536,5120]{1,0:T(8,128)} fusion(bf16[256,5120]{1,0:T(8,128)(2,1)S(1)} %fusion.8, bf16[256,384]{1,0:T(8,128)(2,1)S(1)} %copy-done.7, bf16[256,384]{1,0:T(8,128)(2,1)S(1)} %get-tuple-element.13, bf16[256,384]{1,0:T(8,128)(2,1)S(1)} %copy-done.6, bf16[256,384]{1,0:T(8,128)(2,1)S(1)} %get-tuple-element.12), kind=kOutput, calls=%fused_computation.52 | convolution fusion | flops 4029677568 | bytes 34865152 | tf_op jit(solution)/shard_map/dot_general | solution.py:82
  142.8 47.7 %reduce-scatter.10.cloned.1.call-done = f32[192,1152]{1,0:T(8,128)} async-done(((f32[1536,1152]{1,0:T(8,128)}), f32[192,1152]{1,0:T(8,128)}) %reduce-scatter.10.cloned.1.call-update) | async-done | bytes 884752
  190.5 1.5 copy.16
  192.1 192.4 %reduce-scatter.8.cloned.1.call-done = f32[192,5120]{1,0:T(8,128)} async-done(((f32[1536,5120]{1,0:T(8,128)}), f32[192,5120]{1,0:T(8,128)}) %reduce-scatter.8.cloned.1.call-update) | async-done | bytes 3932176 | tf_op jit(solution)/shard_map/reduce_scatter | solution.py:85
  384.4 3.7 multiply_reduce_fusion
  389.4 39.5 %psum.7 = f32[]{:T(128)} all-reduce(f32[]{:T(128)} %multiply_reduce_fusion), channel_id=1, replica_groups=mesh['sec'=2,'seq'=4,'trk'=4] {'sec','seq','trk'}, use_global_device_ids=true, to_apply=%region_5.6 | all-reduce | flops 1 | bytes 8 | tf_op jit(solution)/shard_map/psum | solution.py:105
  429.7 2.6 multiply_bitcast_fusion
  432.2 2.6 copy.20
  (55 shorter events, 10.2 us)
Async XLA Ops:
  7.2 9.3 %copy-start.9 = (s32[1,40]{1,0:T(1,128)S(1)}, s32[1,40]{1,0:T(1,128)}, u32[]{:S(2)}) copy-start(s32[1,40]{1,0:T(1,128)} %param.12) | copy-start | bytes 484
  7.2 9.4 %copy-start.10 = (s32[4]{0:T(128)S(1)}, s32[4]{0:T(128)}, u32[]{:S(2)}) copy-start(s32[4]{0:T(128)} %param.13) | copy-start | bytes 52
  7.2 103.3 %reduce-scatter.6.cloned.1.call-start = ((), (), s32[]{:S(2)}) async-start(), calls=%async_computation.3 | async-start | bytes 1966080 | tf_op jit(solution)/shard_map/reduce_scatter | solution.py:92
  9.3 11.0 %copy-start.5 = (bf16[4,64,1,40,128]{4,3,2,1,0:T(8,128)(2,1)S(1)}, bf16[4,64,1,40,128]{4,3,2,1,0:T(8,128)(2,1)}, u32[]{:S(2)}) copy-start(bf16[4,64,1,40,128]{4,3,2,1,0:T(8,128)(2,1)} %param.11) | copy-start | bytes 7864324
  11.3 14.5 %copy-start = (bf16[4,64,1536]{2,1,0:T(8,128)(2,1)}, bf16[4,64,1536]{2,1,0:T(8,128)(2,1)S(1)}, u32[]{:S(2)}) copy-start(bf16[4,64,1536]{2,1,0:T(8,128)(2,1)S(1)} %fusion.15) | copy-start | bytes 2359300
  12.2 12.1 %collective-permute-start = (bf16[4,16,1536]{2,1,0:T(8,128)(2,1)}, bf16[4,16,1536]{2,1,0:T(8,128)(2,1)}, u32[]{:S(2)}, u32[]{:S(2)}) collective-permute-start(bf16[4,16,1536]{2,1,0:T(8,128)(2,1)} %get-tuple-element.18), channel_id=1, source_target_pairs={{0,4},{4,8},{8,12},{1,5},{5,9},{9,13},{2,6},{6,10},{10,14},{3,7},{... | collective-permute-start | bytes 589832 | tf_op jit(solution)/shard_map/ppermute | solution.py:23
  15.2 9.1 %collective-permute-start.1 = (bf16[4,16,1536]{2,1,0:T(8,128)(2,1)}, bf16[4,16,1536]{2,1,0:T(8,128)(2,1)}, u32[]{:S(2)}, u32[]{:S(2)}) collective-permute-start(bf16[4,16,1536]{2,1,0:T(8,128)(2,1)} %get-tuple-element.19), channel_id=1, source_target_pairs={{4,0},{8,4},{12,8},{5,1},{9,5},{13,9},{6,2},{10,6},{14,10},{7,3},{... | collective-permute-start | bytes 589832 | tf_op jit(solution)/shard_map/ppermute | solution.py:25
  23.2 28.2 %slice-start = ((s8[5242880]{0:T(1024)(128)(4,1)}), s8[4194304]{0:T(1024)(128)(4,1)S(1)}, s32[]{:S(2)}) async-start(s8[5242880]{0:T(1024)(128)(4,1)} %bitcast.92), calls=%async_computation.6 | async-start | bytes 8388608
  24.3 4.0 copy-start.8
  25.8 4.4 copy-start.1
  25.8 4.4 copy-start.4
  25.8 25.6 %slice-start.1 = ((s8[5242880]{0:T(1024)(128)(4,1)}), s8[1048576]{0:T(1024)(128)(4,1)S(1)}, s32[]{:S(2)}) async-start(s8[5242880]{0:T(1024)(128)(4,1)} %bitcast.92), calls=%async_computation.7 | async-start | bytes 2097152
  73.2 117.3 %reduce-scatter.10.cloned.1.call-start = ((), (), s32[]{:S(2)}) async-start(), calls=%async_computation.5 | async-start | bytes 7962624
  110.5 1.8 copy-start.3
  112.3 1.7 copy-start.2
  125.9 0.9 copy-start.6
  125.9 1.0 copy-start.7
  125.9 258.5 %reduce-scatter.8.cloned.1.call-start = ((), (), s32[]{:S(2)}) async-start(), calls=%async_computation.4 | async-start | bytes 35389440 | tf_op jit(solution)/shard_map/reduce_scatter | solution.py:85
Sparse Core Ops, SparseCore 0:
  73.3 37.1 reduce-scatter.5
  126.0 64.4 reduce-scatter.9
  194.6 189.7 reduce-scatter.7

commit v2 on v1

--- a/solution.py
+++ b/solution.py
@@ -10,7 +10,8 @@
 DILATION_BINS = 16
 HTILES = 60
 GRAD_CLIP = 0.1
-SEND = jnp.float32
+SEND = jnp.bfloat16
+CORES = 2
 
 
 def padded(cells, axis, dim, width):
@@ -39,6 +40,76 @@
     return (live[:, :, None] & valid[None]).astype(jnp.float32)
 
 
+def shift_seq(cells, offset):
+    count = lax.axis_size("seq")
+    return lax.ppermute(
+        cells, "seq", [(i, (i + offset * CORES) % count) for i in range(count)]
+    )
+
+
+def shift_axis(cells, axis, offset):
+    count = lax.axis_size(axis)
+    return lax.ppermute(cells, axis, [(i, (i + offset) % count) for i in range(count)])
+
+
+def from_mate(cells):
+    return lax.ppermute(cells, "seq", [(i, i ^ 1) for i in range(lax.axis_size("seq"))])
+
+
+def with_mate(cells):
+    return jnp.concatenate([cells, from_mate(cells)], axis=0)
+
+
+def core_columns(cells):
+    groups = lax.axis_size("sec") * (lax.axis_size("seq") // CORES)
+    split = cells.reshape(cells.shape[0], groups, CORES, -1)
+    core = lax.rem(lax.axis_index("seq"), CORES)
+    mine = lax.dynamic_index_in_dim(split, core, 2, keepdims=False)
+    other = lax.dynamic_index_in_dim(split, 1 - core, 2, keepdims=False)
+    both = jnp.concatenate([mine, from_mate(other)], axis=0)
+    return both.reshape(both.shape[0], lax.axis_size("sec"), -1, both.shape[-1])
+
+
+def reduced_product(left, right, chips_first):
+    place = {
+        1: (lax.axis_index("sec"), lax.axis_size("sec"), lambda c, k: shift_axis(c, "sec", k)),
+        2: (lax.axis_index("seq") // CORES, lax.axis_size("seq") // CORES, shift_seq),
+    }
+    first, second = (2, 1) if chips_first else (1, 2)
+    here, count, send = place[first]
+
+    def product(index):
+        part = lax.dynamic_index_in_dim(left, index, first, keepdims=False)
+        out = lax.dot_general(
+            part.reshape(part.shape[0], -1),
+            right,
+            (((0,), (0,)), ((), ())),
+            preferred_element_type=jnp.float32,
+        )
+        return out.reshape(part.shape[1], part.shape[2], -1)
+
+    arrived = [
+        send(product(lax.rem(here + k, count)).astype(SEND), k) for k in range(1, count)
+    ]
+    total = product(here)
+    for block in arrived:
+        total = total + block.astype(jnp.float32)
+    here, count, send = place[second]
+    arrived = [
+        send(
+            lax.dynamic_index_in_dim(
+                total, lax.rem(here + k, count), 0, keepdims=False
+            ).astype(SEND),
+            k,
+        )
+        for k in range(1, count)
+    ]
+    total = lax.dynamic_index_in_dim(total, here, 0, keepdims=False)
+    for block in arrived:
+        total = total + block.astype(jnp.float32)
+    return total
+
+
 def body(tokens, norm_gain, dilated_conv_weight, head_weight, targets, owner_tiles, species):
     samples, bins, width = tokens.shape
     taps = dilated_conv_weight.shape[1]
@@ -79,33 +150,45 @@
     spread = jnp.broadcast_to(mask * grad_scale, (samples, bins, columns)).reshape(rows, columns)
     delta = (spread * (softplus - wanted) * sigmoid).astype(jnp.bfloat16)
 
-    raw = lax.dot_general(
-        mixed, delta, (((0,), (0,)), ((), ())), preferred_element_type=jnp.float32
-    ).astype(SEND)
-    raw = lax.psum_scatter(raw, ("sec", "seq"), scatter_dimension=0, tiled=True)
-    raw = raw.astype(jnp.float32)
-
     back = lax.dot_general(
         delta, weights, (((1,), (1,)), ((), ())), preferred_element_type=jnp.float32
     )
     back = jnp.stack([back[:, g * out_share : (g + 1) * out_share] for g in range(owners)])
-    back = lax.psum_scatter(back, "trk", scatter_dimension=0, tiled=True)[0].astype(jnp.bfloat16)
-    conv_part = jnp.concatenate(
+    me = lax.axis_index("trk")
+    arrived = [
+        shift_axis(
+            lax.dynamic_index_in_dim(back, lax.rem(me + k, owners), 0, keepdims=False).astype(SEND),
+            "trk",
+            k,
+        )
+        for k in range(1, owners)
+    ]
+    back = lax.dynamic_index_in_dim(back, me, 0, keepdims=False)
+    for block in arrived:
+        back = back + block.astype(jnp.float32)
+    back = with_mate(back.astype(jnp.bfloat16))
+
+    delta = with_mate(delta)
+    left = core_columns(mixed)
+    half = columns // 2
+    raw = [
+        reduced_product(left, delta[:, :half], True),
+        reduced_product(left, delta[:, half:], False),
+    ]
+    conv_grad = jnp.stack(
         [
-            lax.dot_general(
-                shifted[k], back, (((0,), (0,)), ((), ())), preferred_element_type=jnp.float32
-            )
+            reduced_product(core_columns(shifted[k]), back, k % 2 == 0)
             for k in range(taps)
         ],
         axis=1,
-    ).astype(SEND)
-    conv_grad = lax.psum_scatter(conv_part, ("sec", "seq"), scatter_dimension=0, tiled=True)
-    conv_grad = conv_grad.astype(jnp.float32).reshape(-1, taps, out_share)
-
-    total_sq = lax.psum(jnp.sum(raw * raw), ("sec", "seq", "trk"))
+    )
+
+    total_sq = lax.psum(sum(jnp.sum(r * r) for r in raw), ("sec", "seq", "trk"))
     entries = width * owners * columns
     factor = jnp.minimum(1.0, GRAD_CLIP * lax.rsqrt(total_sq / entries + 1e-06))
-    head_grad = (raw * factor).reshape(-1, 1, slots, lanes)
+    head_grad = jnp.concatenate(
+        [(r * factor).reshape(-1, 1, slots // 2, lanes) for r in raw], axis=2
+    )
     return conv_grad, head_grad
 
 

time: 442 us -> 293 us (0.66)
  waiting for transfers between devices: 277 us -> 75.5 us
  local copies, waits for them, and re-layouts: 17.4 us -> 56.4 us
  starting transfers between devices: 4.64 us -> 26.2 us
  between operations: 14.7 us -> 3.03 us
  other arithmetic: 20.1 us -> 25 us
    reduce_scatter x2 -> x0, waiting for transfers between devices: 230 us -> none  [the longest x1 192 us: body(): raw = lax.psum_scatter(raw, ('sec', 'seq'), scatter_dimension=0, tiled=True)]
    ppermute x0 -> x19, waiting for transfers between devices: none -> 75.5 us  [the longest x5 38.7 us: shift_seq(): lax.ppermute(cells, 'seq', [(i, (i + offset * CORES) % count) for i in ra...]
    unnamed x4 -> x0, waiting for transfers between devices: 47.8 us -> none
    dynamic_slice x0 -> x8, local copies, waits for them, and re-layouts: none -> 31.3 us  [the longest x5 20.9 us: core_columns(): other = lax.dynamic_index_in_dim(split, 1 - core, 2, keepdims=False)]
    ppermute x0 -> x19, starting transfers between devices: none -> 22.6 us  [the longest x5 10.5 us: shift_seq(): lax.ppermute(cells, 'seq', [(i, (i + offset * CORES) % count) for i in ra...]
    unnamed x31 -> x51, local copies, waits for them, and re-layouts: 14.3 us -> 2.36 us
    another operation x0 -> x3, local copies, waits for them, and re-layouts: none -> 7.93 us  [core_columns(): split = cells.reshape(cells.shape[0], groups, CORES, -1)]
    slice x1 -> x5, local copies, waits for them, and re-layouts: 0.83 us -> 7.79 us  [body(): mixed = jnp.concatenate([gathered[g] for g in range(owners)], axis=-1)]
  transfers between devices with their start and end apart: 5 -> 21, of which waited for: 3 -> 5; matrix products, arithmetic and copies ran while one was open for 6% -> 30% of each run, Pallas kernels for 0% -> 0%
where the time goes in v2:
time: 293 us; the launch traced here: 291 us
  waiting for transfers between devices  75.5 us (26%)
  blocking collectives  57.2 us (20%)
  local copies, waits for them, and re-layouts  56.4 us (19%)
  matrix products  47.5 us (16%)
  starting transfers between devices  26.2 us (9%)
  other arithmetic  25 us (9%)
  between operations  3.03 us (1%)
    ppermute x5, waiting for transfers between devices, shift_seq(): lax.ppermute(cells, 'seq', [(i, (i + offset * CORES) % count) for i in ra...  38.7 us
    psum x1, blocking collectives, body(): lax.psum(sum((jnp.sum(r * r) for r in raw)), ('sec', 'seq', 'trk'))  37.8 us
    ppermute x8, waiting for transfers between devices, shift_axis(): lax.ppermute(cells, axis, [(i, (i + offset) % count) for i in range(count)])  36.8 us
    dot_general x10, matrix products, product(): lax.dot_general(part.reshape(part.shape[0], -1), right, (((0,), (0,)), ((...  20.9 us
    dynamic_slice x5, local copies, waits for them, and re-layouts, core_columns(): other = lax.dynamic_index_in_dim(split, 1 - core, 2, keepdims=False)  20.9 us
    all_gather x1, blocking collectives, body(): gathered = lax.all_gather(mixed_share, 'trk', axis=0)  19.4 us
    dot_general x1, matrix products, body(): logits = jnp.dot(mixed, weights, preferred_element_type=jnp.float32)  12.7 us
    ppermute x5, starting transfers between devices, shift_seq(): lax.ppermute(cells, 'seq', [(i, (i + offset * CORES) % count) for i in ra...  10.5 us
  transfers between devices with their start and end apart: 21, of which 5 were waited for; matrix products, arithmetic and copies ran while one was open for 30% of the time, Pallas kernels for 0%

profile of v2, /device:TPU:0, one launch (start us, length us, event | category | flops | bytes accessed | tf_op | source)
XLA Modules:
  0.0 290.8 jit_solution(18189717369866905010)
XLA Ops:
  11.4 4.7 %convert.4 = f32[32,8,40,128]{3,2,1,0:T(8,128)} convert(bf16[32,8,40,128]{3,2,1,0:T(8,128)(2,1)} %bitcast.242) | non-fusion elementwise | flops 1310720 | bytes 7864320
  23.4 19.4 %all-gather = bf16[1024,384]{1,0:T(8,128)(2,1)S(1)} all-gather(bf16[256,384]{1,0:T(8,128)(2,1)S(1)} %fusion.36), channel_id=2, replica_groups=mesh['sec'=2,'seq'=4,'trk'=4] {'trk'}, dimensions={0}, use_global_device_ids=true | all-gather | bytes 983040 | tf_op jit(solution)/shard_map/all_gather | solution.py:137
  44.4 12.7 %fusion.8 = bf16[256,5120]{1,0:T(8,128)(2,1)S(1)} fusion(f32[32,8,40,128]{3,2,1,0:T(8,128)S(1)} %bitcast.232, f32[4,5120]{1,0:T(4,128)} %fusion.94, bf16[192,8,40,128]{3,2,1,0:T(8,128)(2,1)} %bitcast.233, bf16[256,384]{1,0:T(8,128)(2,1)S(1)} %get-tuple-element.22, bf16[256,384]{1,0:T(8,128)(2,1)} %get-tuple-element.20, ...), kind=kOutput, calls=%fused_computation.9 | convolution fusion | flops 4045406208 | bytes 24461312 | tf_op jit(solution)/shard_map/dot_general | solution.py:145
  65.3 4.2 %reshape_reshape.9 = bf16[256,4,2,192]{3,2,1,0:T(2,128)(2,1)} reshape(bf16[4,64,1536]{2,1,0:T(8,128)(2,1)} %copy-done.6) | data formatting | bytes 1572864 | tf_op jit(solution)/shard_map/reshape;reshape | solution.py:65
  73.8 5.5 %constant_dynamic-slice_fusion.1 = (bf16[256,4,1,192]{3,2,1,0:T(2,128)(2,1)}, bf16[256,4,1,192]{3,2,1,0:T(2,128)(2,1)}, bf16[256,4,1,192]{3,2,1,0:T(2,128)(2,1)}, bf16[256,4,1,192]{3,2,1,0:T(2,128)(2,1)}) fusion(bf16[256,4,2,192]{3,2,1,0:T(2,128)(2,1)S(1)} %copy-done.5, s32[]{:T(128)S(6)} %select_n.91, s32[]{:T(128)S(6)} %select_n.90, ...), kind=kLoop, calls=%fused_computation.155 | loop fusion | bytes 3145736 | tf_op jit(solution)/shard_map/jit(dynamic_index_in_dim)/dynamic_slice | solution.py:68
  79.3 3.4 %copy.16 = bf16[256,4,1,192]{0,3,2,1:T(8,128)(2,1)} copy(bf16[256,4,1,192]{3,2,1,0:T(2,128)(2,1)} %get-tuple-element.15) | data formatting | bytes 786432 | tf_op jit(solution)/shard_map/jit(dynamic_index_in_dim)/dynamic_slice | solution.py:68
  83.1 7.8 %fusion = f32[256,1536]{1,0:T(8,128)S(1)} fusion(bf16[256,5120]{1,0:T(8,128)(2,1)S(1)} %fusion.8, bf16[192,8,40,128]{3,2,1,0:T(8,128)(2,1)} %bitcast.234), kind=kOutput, calls=%fused_computation | convolution fusion | flops 4026531840 | bytes 19922944 | tf_op jit(solution)/shard_map/dot_general | solution.py:153
  91.5 3.6 %collective-permute-start.5 = (bf16[256,384]{1,0:T(8,128)(2,1)S(1)}, bf16[256,384]{1,0:T(8,128)(2,1)S(1)}, u32[]{:S(2)}, u32[]{:S(2)}) collective-permute-start(bf16[256,384]{1,0:T(8,128)(2,1)S(1)} %get-tuple-element.5), channel_id=1, source_target_pairs={{0,3},{1,0},{2,1},{3,2},{4,7},{5,4},{6,5},{7,6},{8,11},{9,8},{10,9... | collective-permute-start | bytes 589832 | tf_op jit(solution)/shard_map/ppermute | solution.py:52
  95.9 3.9 %convolution_convert_fusion = bf16[2,192,2560]{2,1,0:T(8,128)(2,1)} fusion(s32[]{:T(128)S(6)} %select_n.104, bf16[256,2,2,192]{0,3,2,1:T(8,128)(2,1)S(1)} %bitcast.237, bf16[256,2,2,192]{0,3,2,1:T(8,128)(2,1)} %bitcast.243, bf16[256,5120]{1,0:T(8,128)(2,1)} %collective-permute-done.16, bf16[256,5120]{1,0:T(8,128)(2,1)S(1)} %fusion.8), kind=kOutput, calls=%fused_computation.14 | convolution fusion | flops 1013645312 | bytes 7995396 | tf_op jit(solution)/shard_map/dot_general | solution.py:83
  102.7 9.1 %collective-permute-done.4 = bf16[256,384]{1,0:T(8,128)(2,1)S(1)} collective-permute-done((bf16[256,384]{1,0:T(8,128)(2,1)S(1)}, bf16[256,384]{1,0:T(8,128)(2,1)S(1)}, u32[]{:S(2)}, u32[]{:S(2)}) %collective-permute-start.4) | collective-permute-done | bytes 196640 | tf_op jit(solution)/shard_map/ppermute | solution.py:52
  114.5 5.0 %constant_dynamic-slice_fusion.3 = (bf16[256,4,1,192]{3,2,1,0:T(2,128)(2,1)}, bf16[256,4,1,192]{3,2,1,0:T(2,128)(2,1)}) fusion(bf16[256,4,2,192]{3,2,1,0:T(2,128)(2,1)} %reshape_reshape.10, s32[]{:T(128)S(6)} %select_n.91, s32[]{:T(128)S(6)} %select_n.90), kind=kLoop, calls=%fused_computation.159 | loop fusion | bytes 1572872 | tf_op jit(solution)/shard_map/jit(dynamic_index_in_dim)/dynamic_slice | solution.py:68
  119.5 3.4 %copy.14 = bf16[256,4,1,192]{0,3,2,1:T(8,128)(2,1)} copy(bf16[256,4,1,192]{3,2,1,0:T(2,128)(2,1)} %get-tuple-element.13) | data formatting | bytes 786432 | tf_op jit(solution)/shard_map/jit(dynamic_index_in_dim)/dynamic_slice | solution.py:68
  123.5 3.4 %copy.13 = bf16[256,4,1,192]{0,3,1,2:T(8,128)(2,1)} copy(bf16[256,4,1,192]{3,2,1,0:T(2,128)(2,1)} %get-tuple-element.14) | data formatting | bytes 786432 | tf_op jit(solution)/shard_map/jit(dynamic_index_in_dim)/dynamic_slice | solution.py:67
  126.9 3.4 %copy.15 = bf16[256,4,1,192]{0,3,1,2:T(8,128)(2,1)} copy(bf16[256,4,1,192]{3,2,1,0:T(2,128)(2,1)} %get-tuple-element.16) | data formatting | bytes 786432 | tf_op jit(solution)/shard_map/jit(dynamic_index_in_dim)/dynamic_slice | solution.py:67
  130.4 3.5 %copy.11 = bf16[256,4,1,192]{0,3,1,2:T(8,128)(2,1)} copy(bf16[256,4,1,192]{3,2,1,0:T(2,128)(2,1)} %get-tuple-element.29) | data formatting | bytes 786432 | tf_op jit(solution)/shard_map/jit(dynamic_index_in_dim)/dynamic_slice | solution.py:67
  133.9 3.5 %copy.12 = bf16[256,4,1,192]{0,3,2,1:T(8,128)(2,1)} copy(bf16[256,4,1,192]{3,2,1,0:T(2,128)(2,1)} %get-tuple-element.30) | data formatting | bytes 786432 | tf_op jit(solution)/shard_map/jit(dynamic_index_in_dim)/dynamic_slice | solution.py:68
  139.0 4.2 %collective-permute-start.13 = (bf16[2,192,384]{2,1,0:T(8,128)(2,1)S(1)}, bf16[2,192,384]{2,1,0:T(8,128)(2,1)S(1)}, u32[]{:S(2)}, u32[]{:S(2)}) collective-permute-start(bf16[2,192,384]{2,1,0:T(8,128)(2,1)S(1)} %convolution_convert_fusion.2), channel_id=1, source_target_pairs={{0,8},{4,12},{8,0},{12,4},{1,9},{5,13},{9,1},{13,5},{2,10},{6,14},... | collective-permute-start | bytes 884744 | tf_op jit(solution)/shard_map/ppermute | solution.py:45
  160.8 38.7 %collective-permute-done.7 = bf16[2,192,384]{2,1,0:T(8,128)(2,1)S(1)} collective-permute-done((bf16[2,192,384]{2,1,0:T(8,128)(2,1)S(1)}, bf16[2,192,384]{2,1,0:T(8,128)(2,1)S(1)}, u32[]{:S(2)}, u32[]{:S(2)}) %collective-permute-start.7) | collective-permute-done | bytes 294944 | tf_op jit(solution)/shard_map/ppermute | solution.py:45
  200.9 3.1 %convolution_add_fusion = f32[2,192,2560]{2,1,0:T(8,128)S(1)} fusion(bf16[2,192,2560]{2,1,0:T(8,128)(2,1)} %collective-permute-done.19, s32[]{:T(128)S(6)} %select_n.103, bf16[256,2,2,192]{0,3,2,1:T(8,128)(2,1)S(1)} %bitcast.239, bf16[256,2,2,192]{0,3,2,1:T(8,128)(2,1)S(1)} %bitcast.245, bf16[256,5120]{1,0:T(8,128)(2,1)} %collective-permute-done.16, ...), kind=kOutput, calls=%fused_computation.12 | convolution fusion | flops 1014628352 | bytes 11927556 | tf_op jit(solution)/shard_map/dot_general | solution.py:83
  211.1 23.6 %collective-permute-done.8 = bf16[192,384]{1,0:T(8,128)(2,1)S(1)} collective-permute-done((bf16[192,384]{1,0:T(8,128)(2,1)S(1)}, bf16[192,384]{1,0:T(8,128)(2,1)S(1)}, u32[]{:S(2)}, u32[]{:S(2)}) %collective-permute-start.8) | collective-permute-done | bytes 147488 | tf_op jit(solution)/shard_map/ppermute | solution.py:52
  239.3 37.8 %psum.7 = f32[]{:T(128)} all-reduce(f32[]{:T(128)S(6)} %add.239), channel_id=1, replica_groups=mesh['sec'=2,'seq'=4,'trk'=4] {'sec','seq','trk'}, use_global_device_ids=true, to_apply=%region_3.4 | all-reduce | flops 1 | bytes 8 | tf_op jit(solution)/shard_map/psum | solution.py:186
  277.7 4.7 %fusion.24 = (f32[192,2560]{1,0:T(8,128)}, f32[192,2560]{1,0:T(8,128)}) fusion(bf16[192,2560]{1,0:T(8,128)(2,1)S(1)} %collective-permute-done.18, f32[2,192,2560]{2,1,0:T(8,128)} %copy-done.1, s32[]{:T(128)S(6)} %select_n.103, f32[]{:T(128)S(6)} %min.3, bf16[192,2560]{1,0:T(8,128)(2,1)S(1)} %copy-done.8, f32[2,192,2560]{2,1,0:T(8,128)} %copy-done, ...), kind=kLoop, calls=%fused_computation.44 | loop fusion | flops 2949120 | bytes 9830412 | tf_op jit(solution)/shard_map/mul | solution.py:190
  284.0 2.8 reshape.268
  286.8 4.0 %maximum_bitcast_fusion = f32[192,1,40,128]{3,2,1,0:T(8,128)} fusion(f32[192,1,20,128]{3,2,0,1:T(8,128)} %reshape.268, f32[192,1,20,128]{3,2,0,1:T(8,128)S(1)} %reshape.267), kind=kLoop, calls=%fused_computation.16 | loop fusion | flops 983040 | bytes 7864320
  (141 shorter events, 72.2 us)
Async XLA Ops:
  4.6 12.6 %collective-permute-start = (bf16[4,16,1536]{2,1,0:T(8,128)(2,1)S(1)}, bf16[4,16,1536]{2,1,0:T(8,128)(2,1)S(1)}, u32[]{:S(2)}, u32[]{:S(2)}) collective-permute-start(bf16[4,16,1536]{2,1,0:T(8,128)(2,1)S(1)} %get-tuple-element.25), channel_id=1, source_target_pairs={{0,4},{4,8},{8,12},{1,5},{5,9},{9,13},{2,6},{6,10},{10,14},{3,7},{... | collective-permute-start | bytes 589832 | tf_op jit(solution)/shard_map/ppermute | solution.py:24
  7.0 10.9 %collective-permute-start.2 = (bf16[4,16,1536]{2,1,0:T(8,128)(2,1)S(1)}, bf16[4,16,1536]{2,1,0:T(8,128)(2,1)}, u32[]{:S(2)}, u32[]{:S(2)}) collective-permute-start(bf16[4,16,1536]{2,1,0:T(8,128)(2,1)S(1)} %get-tuple-element.26), channel_id=1, source_target_pairs={{4,0},{8,4},{12,8},{5,1},{9,5},{13,9},{6,2},{10,6},{14,10},{7,3},{... | collective-permute-start | bytes 589832 | tf_op jit(solution)/shard_map/ppermute | solution.py:26
  16.1 28.3 %slice-start = ((s8[5242880]{0:T(1024)(128)(4,1)}), s8[4194304]{0:T(1024)(128)(4,1)S(1)}, s32[]{:S(2)}) async-start(s8[5242880]{0:T(1024)(128)(4,1)} %bitcast.231), calls=%async_computation | async-start | bytes 8388608
  57.1 38.0 %collective-permute-start.16 = (bf16[256,5120]{1,0:T(8,128)(2,1)S(1)}, bf16[256,5120]{1,0:T(8,128)(2,1)}, u32[]{:S(2)}, u32[]{:S(2)}) collective-permute-start(bf16[256,5120]{1,0:T(8,128)(2,1)S(1)} %fusion.8), channel_id=1, source_target_pairs={{0,4},{4,0},{8,12},{12,8},{1,5},{5,1},{9,13},{13,9},{2,6},{6,2},{1... | collective-permute-start | bytes 7864328 | tf_op jit(solution)/shard_map/ppermute | solution.py:56
  73.7 21.4 %collective-permute-start.15 = (bf16[256,4,192]{0,2,1:T(8,128)(2,1)S(1)}, bf16[256,4,192]{0,2,1:T(8,128)(2,1)S(1)}, u32[]{:S(2)}, u32[]{:S(2)}) collective-permute-start(bf16[256,4,192]{0,2,1:T(8,128)(2,1)S(1)} %get-tuple-element.17), channel_id=1, source_target_pairs={{0,4},{4,0},{8,12},{12,8},{1,5},{5,1},{9,13},{13,9},{2,6},{6,2},{1... | collective-permute-start | bytes 1179656 | tf_op jit(solution)/shard_map/ppermute | solution.py:56
  82.7 54.6 %collective-permute-start.12 = (bf16[256,4,192]{0,2,1:T(8,128)(2,1)}, bf16[256,4,192]{0,2,1:T(8,128)(2,1)}, u32[]{:S(2)}, u32[]{:S(2)}) collective-permute-start(bf16[256,4,192]{0,2,1:T(8,128)(2,1)} %bitcast.48), channel_id=1, source_target_pairs={{0,4},{4,0},{8,12},{12,8},{1,5},{5,1},{9,13},{13,9},{2,6},{6,2},{1... | collective-permute-start | bytes 1179656 | tf_op jit(solution)/shard_map/ppermute | solution.py:56
  91.2 10.1 %collective-permute-start.3 = (bf16[256,384]{1,0:T(8,128)(2,1)S(1)}, bf16[256,384]{1,0:T(8,128)(2,1)S(1)}, u32[]{:S(2)}, u32[]{:S(2)}) collective-permute-start(bf16[256,384]{1,0:T(8,128)(2,1)S(1)} %get-tuple-element.4), channel_id=1, source_target_pairs={{0,1},{1,2},{2,3},{3,0},{4,5},{5,6},{6,7},{7,4},{8,9},{9,10},{10,1... | collective-permute-start | bytes 589832 | tf_op jit(solution)/shard_map/ppermute | solution.py:52
  91.5 11.2 %collective-permute-start.5 = (bf16[256,384]{1,0:T(8,128)(2,1)S(1)}, bf16[256,384]{1,0:T(8,128)(2,1)S(1)}, u32[]{:S(2)}, u32[]{:S(2)}) collective-permute-start(bf16[256,384]{1,0:T(8,128)(2,1)S(1)} %get-tuple-element.5), channel_id=1, source_target_pairs={{0,3},{1,0},{2,1},{3,2},{4,7},{5,4},{6,5},{7,6},{8,11},{9,8},{10,9... | collective-permute-start | bytes 589832 | tf_op jit(solution)/shard_map/ppermute | solution.py:52
  95.1 16.7 %collective-permute-start.4 = (bf16[256,384]{1,0:T(8,128)(2,1)S(1)}, bf16[256,384]{1,0:T(8,128)(2,1)S(1)}, u32[]{:S(2)}, u32[]{:S(2)}) collective-permute-start(bf16[256,384]{1,0:T(8,128)(2,1)S(1)} %get-tuple-element.6), channel_id=1, source_target_pairs={{0,2},{1,3},{2,0},{3,1},{4,6},{5,7},{6,4},{7,5},{8,10},{9,11},{10,... | collective-permute-start | bytes 589832 | tf_op jit(solution)/shard_map/ppermute | solution.py:52
  99.8 101.1 %collective-permute-start.19 = (bf16[2,192,2560]{2,1,0:T(8,128)(2,1)}, bf16[2,192,2560]{2,1,0:T(8,128)(2,1)}, u32[]{:S(2)}, u32[]{:S(2)}) collective-permute-start(bf16[2,192,2560]{2,1,0:T(8,128)(2,1)} %convolution_convert_fusion), channel_id=1, source_target_pairs={{0,16},{16,0},{1,17},{17,1},{2,18},{18,2},{3,19},{19,3},{4,20},{20... | collective-permute-start | bytes 5898248 | tf_op jit(solution)/shard_map/ppermute | solution.py:52
  112.6 24.8 %collective-permute-start.6 = (bf16[256,384]{1,0:T(8,128)(2,1)}, bf16[256,384]{1,0:T(8,128)(2,1)}, u32[]{:S(2)}, u32[]{:S(2)}) collective-permute-start(bf16[256,384]{1,0:T(8,128)(2,1)} %fusion.80), channel_id=1, source_target_pairs={{0,4},{4,0},{8,12},{12,8},{1,5},{5,1},{9,13},{13,9},{2,6},{6,2},{1... | collective-permute-start | bytes 589832 | tf_op jit(solution)/shard_map/ppermute | solution.py:56
  122.9 22.9 %collective-permute-start.9 = (bf16[256,4,192]{0,2,1:T(8,128)(2,1)}, bf16[256,4,192]{0,2,1:T(8,128)(2,1)}, u32[]{:S(2)}, u32[]{:S(2)}) collective-permute-start(bf16[256,4,192]{0,2,1:T(8,128)(2,1)} %bitcast.36), channel_id=1, source_target_pairs={{0,4},{4,0},{8,12},{12,8},{1,5},{5,1},{9,13},{13,9},{2,6},{6,2},{1... | collective-permute-start | bytes 1179656 | tf_op jit(solution)/shard_map/ppermute | solution.py:56
  137.3 11.6 %collective-permute-start.1 = (bf16[256,4,192]{0,2,1:T(8,128)(2,1)}, bf16[256,4,192]{0,2,1:T(8,128)(2,1)S(1)}, u32[]{:S(2)}, u32[]{:S(2)}) collective-permute-start(bf16[256,4,192]{0,2,1:T(8,128)(2,1)} %bitcast.258), channel_id=1, source_target_pairs={{0,4},{4,0},{8,12},{12,8},{1,5},{5,1},{9,13},{13,9},{2,6},{6,2},{1... | collective-permute-start | bytes 1179656 | tf_op jit(solution)/shard_map/ppermute | solution.py:56
  139.0 13.4 %collective-permute-start.13 = (bf16[2,192,384]{2,1,0:T(8,128)(2,1)S(1)}, bf16[2,192,384]{2,1,0:T(8,128)(2,1)S(1)}, u32[]{:S(2)}, u32[]{:S(2)}) collective-permute-start(bf16[2,192,384]{2,1,0:T(8,128)(2,1)S(1)} %convolution_convert_fusion.2), channel_id=1, source_target_pairs={{0,8},{4,12},{8,0},{12,4},{1,9},{5,13},{9,1},{13,5},{2,10},{6,14},... | collective-permute-start | bytes 884744 | tf_op jit(solution)/shard_map/ppermute | solution.py:45
  145.7 60.5 %collective-permute-start.17 = (bf16[2,192,2560]{2,1,0:T(8,128)(2,1)S(1)}, bf16[2,192,2560]{2,1,0:T(8,128)(2,1)S(1)}, u32[]{:S(2)}, u32[]{:S(2)}) collective-permute-start(bf16[2,192,2560]{2,1,0:T(8,128)(2,1)S(1)} %convolution_convert_fusion.1), channel_id=1, source_target_pairs={{0,8},{4,12},{8,0},{12,4},{1,9},{5,13},{9,1},{13,5},{2,10},{6,14},... | collective-permute-start | bytes 5898248 | tf_op jit(solution)/shard_map/ppermute | solution.py:45
  147.3 9.8 %collective-permute-start.10 = (bf16[2,192,384]{2,1,0:T(8,128)(2,1)S(1)}, bf16[2,192,384]{2,1,0:T(8,128)(2,1)S(1)}, u32[]{:S(2)}, u32[]{:S(2)}) collective-permute-start(bf16[2,192,384]{2,1,0:T(8,128)(2,1)S(1)} %convolution_convert_fusion.3), channel_id=1, source_target_pairs={{0,16},{16,0},{1,17},{17,1},{2,18},{18,2},{3,19},{19,3},{4,20},{20... | collective-permute-start | bytes 884744 | tf_op jit(solution)/shard_map/ppermute | solution.py:52
  150.3 49.1 %collective-permute-start.7 = (bf16[2,192,384]{2,1,0:T(8,128)(2,1)S(1)}, bf16[2,192,384]{2,1,0:T(8,128)(2,1)S(1)}, u32[]{:S(2)}, u32[]{:S(2)}) collective-permute-start(bf16[2,192,384]{2,1,0:T(8,128)(2,1)S(1)} %convolution_convert_fusion.4), channel_id=1, source_target_pairs={{0,8},{4,12},{8,0},{12,4},{1,9},{5,13},{9,1},{13,5},{2,10},{6,14},... | collective-permute-start | bytes 884744 | tf_op jit(solution)/shard_map/ppermute | solution.py:45
  153.9 57.2 %collective-permute-start.14 = (bf16[192,384]{1,0:T(8,128)(2,1)S(1)}, bf16[192,384]{1,0:T(8,128)(2,1)S(1)}, u32[]{:S(2)}, u32[]{:S(2)}) collective-permute-start(bf16[192,384]{1,0:T(8,128)(2,1)S(1)} %fusion.93), channel_id=1, source_target_pairs={{0,16},{16,0},{1,17},{17,1},{2,18},{18,2},{3,19},{19,3},{4,20},{20... | collective-permute-start | bytes 442376 | tf_op jit(solution)/shard_map/ppermute | solution.py:52
  158.6 52.4 %collective-permute-start.11 = (bf16[192,384]{1,0:T(8,128)(2,1)S(1)}, bf16[192,384]{1,0:T(8,128)(2,1)S(1)}, u32[]{:S(2)}, u32[]{:S(2)}) collective-permute-start(bf16[192,384]{1,0:T(8,128)(2,1)S(1)} %fusion.92), channel_id=1, source_target_pairs={{0,8},{4,12},{8,0},{12,4},{1,9},{5,13},{9,1},{13,5},{2,10},{6,14},... | collective-permute-start | bytes 442376 | tf_op jit(solution)/shard_map/ppermute | solution.py:45
  204.0 30.8 %copy-start = (f32[2,192,2560]{2,1,0:T(8,128)}, f32[2,192,2560]{2,1,0:T(8,128)S(1)}, u32[]{:S(2)}) copy-start(f32[2,192,2560]{2,1,0:T(8,128)S(1)} %convolution_add_fusion) | copy-start | bytes 11796484
  204.2 30.6 %collective-permute-start.20 = (bf16[192,2560]{1,0:T(8,128)(2,1)S(1)}, bf16[192,2560]{1,0:T(8,128)(2,1)S(1)}, u32[]{:S(2)}, u32[]{:S(2)}) collective-permute-start(bf16[192,2560]{1,0:T(8,128)(2,1)S(1)} %fusion.40), channel_id=1, source_target_pairs={{0,8},{4,12},{8,0},{12,4},{1,9},{5,13},{9,1},{13,5},{2,10},{6,14},... | collective-permute-start | bytes 2949128 | tf_op jit(solution)/shard_map/ppermute | solution.py:45
  208.8 27.1 %collective-permute-start.18 = (bf16[192,2560]{1,0:T(8,128)(2,1)S(1)}, bf16[192,2560]{1,0:T(8,128)(2,1)S(1)}, u32[]{:S(2)}, u32[]{:S(2)}) collective-permute-start(bf16[192,2560]{1,0:T(8,128)(2,1)S(1)} %fusion.39), channel_id=1, source_target_pairs={{0,16},{16,0},{1,17},{17,1},{2,18},{18,2},{3,19},{19,3},{4,20},{20... | collective-permute-start | bytes 2949128 | tf_op jit(solution)/shard_map/ppermute | solution.py:52
  210.4 24.3 %collective-permute-start.8 = (bf16[192,384]{1,0:T(8,128)(2,1)S(1)}, bf16[192,384]{1,0:T(8,128)(2,1)S(1)}, u32[]{:S(2)}, u32[]{:S(2)}) collective-permute-start(bf16[192,384]{1,0:T(8,128)(2,1)S(1)} %fusion.91), channel_id=1, source_target_pairs={{0,16},{16,0},{1,17},{17,1},{2,18},{18,2},{3,19},{19,3},{4,20},{20... | collective-permute-start | bytes 442376 | tf_op jit(solution)/shard_map/ppermute | solution.py:52
  235.9 41.7 %copy-start.8 = (bf16[192,2560]{1,0:T(8,128)(2,1)S(1)}, bf16[192,2560]{1,0:T(8,128)(2,1)}, u32[]{:S(2)}) copy-start(bf16[192,2560]{1,0:T(8,128)(2,1)} %copy-done.7) | copy-start | bytes 2949124
  (22 other events, 181.9 us)

commit v3 on v2

--- a/solution.py
+++ b/solution.py
@@ -60,38 +60,50 @@
     return jnp.concatenate([cells, from_mate(cells)], axis=0)
 
 
-def core_columns(cells):
-    groups = lax.axis_size("sec") * (lax.axis_size("seq") // CORES)
-    split = cells.reshape(cells.shape[0], groups, CORES, -1)
-    core = lax.rem(lax.axis_index("seq"), CORES)
-    mine = lax.dynamic_index_in_dim(split, core, 2, keepdims=False)
-    other = lax.dynamic_index_in_dim(split, 1 - core, 2, keepdims=False)
-    both = jnp.concatenate([mine, from_mate(other)], axis=0)
-    return both.reshape(both.shape[0], lax.axis_size("sec"), -1, both.shape[-1])
-
-
-def reduced_product(left, right, chips_first):
-    place = {
-        1: (lax.axis_index("sec"), lax.axis_size("sec"), lambda c, k: shift_axis(c, "sec", k)),
-        2: (lax.axis_index("seq") // CORES, lax.axis_size("seq") // CORES, shift_seq),
-    }
-    first, second = (2, 1) if chips_first else (1, 2)
+def picked(cells, chips_first):
+    width = cells.shape[-1]
+    secs, chips = lax.axis_size("sec"), lax.axis_size("seq") // CORES
+    size = width // (secs * chips * CORES)
+    seq = lax.axis_index("seq")
+    place = jnp.arange(width // CORES, dtype=jnp.int32)
+    group = place // size
+    if chips_first:
+        sec = group % secs
+        chip = (group // secs + seq // CORES) % chips
+    else:
+        chip = group % chips
+        sec = (group // chips + lax.axis_index("sec")) % secs
+    source = ((sec * chips + chip) * CORES + seq % CORES) * size + place % size
+    choice = jnp.arange(width, dtype=jnp.int32)[:, None] == source[None, :]
+    return jnp.dot(
+        cells, choice.astype(cells.dtype), preferred_element_type=jnp.float32
+    ).astype(cells.dtype)
+
+
+def reduced_product(pairs, size, chips_first):
+    place = (
+        (lax.axis_index("sec"), lax.axis_size("sec"), lambda c, k: shift_axis(c, "sec", k)),
+        (lax.axis_index("seq") // CORES, lax.axis_size("seq") // CORES, shift_seq),
+    )
+    first, second = (1, 0) if chips_first else (0, 1)
     here, count, send = place[first]
-
-    def product(index):
-        part = lax.dynamic_index_in_dim(left, index, first, keepdims=False)
-        out = lax.dot_general(
-            part.reshape(part.shape[0], -1),
-            right,
-            (((0,), (0,)), ((), ())),
-            preferred_element_type=jnp.float32,
-        )
-        return out.reshape(part.shape[1], part.shape[2], -1)
-
-    arrived = [
-        send(product(lax.rem(here + k, count)).astype(SEND), k) for k in range(1, count)
-    ]
-    total = product(here)
+    inner = place[second][1]
+
+    def product(k):
+        outs = [
+            lax.dot_general(
+                left[:, k * inner * size : (k + 1) * inner * size],
+                right,
+                (((0,), (0,)), ((), ())),
+                preferred_element_type=jnp.float32,
+            )
+            for left, right in pairs
+        ]
+        out = outs[0] if len(outs) == 1 else jnp.concatenate(outs, axis=1)
+        return out.reshape(inner, size, -1)
+
+    arrived = [send(product(k).astype(SEND), k) for k in range(1, count)]
+    total = product(0)
     for block in arrived:
         total = total + block.astype(jnp.float32)
     here, count, send = place[second]
@@ -124,6 +136,7 @@
     normed = inputs * lax.rsqrt(mean_sq + 1e-06) * norm_gain.astype(jnp.float32)
     hidden = jax.nn.gelu(normed).astype(jnp.bfloat16)
     hidden = padded(hidden, "seq", 1, DILATION_BINS)
+    hidden_both = with_mate(hidden)
     shifted = [
         hidden[:, k * DILATION_BINS : k * DILATION_BINS + bins].reshape(rows, width)
         for k in range(taps)
@@ -169,19 +182,30 @@
     back = with_mate(back.astype(jnp.bfloat16))
 
     delta = with_mate(delta)
-    left = core_columns(mixed)
+    both = with_mate(mixed)
+    size = width // (lax.axis_size("sec") * lax.axis_size("seq"))
     half = columns // 2
     raw = [
-        reduced_product(left, delta[:, :half], True),
-        reduced_product(left, delta[:, half:], False),
-    ]
-    conv_grad = jnp.stack(
-        [
-            reduced_product(core_columns(shifted[k]), back, k % 2 == 0)
-            for k in range(taps)
-        ],
-        axis=1,
-    )
+        reduced_product([(picked(both, True), delta[:, :half])], size, True),
+        reduced_product([(picked(both, False), delta[:, half:])], size, False),
+    ]
+    conv_parts = [None] * taps
+    for chips_first in (True, False):
+        chosen = [k for k in range(taps) if (k % 2 == 0) == chips_first]
+        lefts = picked(hidden_both, chips_first)
+        pairs = [
+            (
+                lefts[:, k * DILATION_BINS : k * DILATION_BINS + bins].reshape(
+                    CORES * rows, -1
+                ),
+                back,
+            )
+            for k in chosen
+        ]
+        part = reduced_product(pairs, size, chips_first)
+        for i, k in enumerate(chosen):
+            conv_parts[k] = part[:, i * out_share : (i + 1) * out_share]
+    conv_grad = jnp.stack(conv_parts, axis=1)
 
     total_sq = lax.psum(sum(jnp.sum(r * r) for r in raw), ("sec", "seq", "trk"))
     entries = width * owners * columns

time: 293 us -> 265 us (0.904)
  local copies, waits for them, and re-layouts: 56.4 us -> 19.6 us
  matrix products: 47.5 us -> 57.8 us
  starting transfers between devices: 26.2 us -> 17.4 us
  other arithmetic: 25 us -> 31.7 us
  blocking collectives: 57.2 us -> 62 us
  waiting for transfers between devices: 75.5 us -> 72.3 us
    dynamic_slice x8 -> x0, local copies, waits for them, and re-layouts: 31.3 us -> none  [the longest x5 20.9 us: core_columns(): other = lax.dynamic_index_in_dim(split, 1 - core, 2, keepdims=False)]
    another operation x3 -> x1, local copies, waits for them, and re-layouts: 7.93 us -> 0.04 us  [body(): conv_grad = jnp.stack(conv_parts, axis=1)]
    slice x5 -> x1, local copies, waits for them, and re-layouts: 7.79 us -> 0.08 us  [body(): mixed = jnp.concatenate([gathered[g] for g in range(owners)], axis=-1)]
    ppermute x5 -> x4, waiting for transfers between devices: 38.7 us -> 32 us  [shift_seq(): lax.ppermute(cells, 'seq', [(i, (i + offset * CORES) % count) for i in ra...]
    ppermute x5 -> x4, starting transfers between devices: 10.5 us -> 4.11 us  [shift_seq(): lax.ppermute(cells, 'seq', [(i, (i + offset * CORES) % count) for i in ra...]
    dot_general x10 -> x14, matrix products: 20.9 us -> 26.7 us  [the longest x10 15.1 us: product(): lax.dot_general(left[:, k * inner * size:(k + 1) * inner * size], right,...]
    concatenate x0 -> x2, local copies, waits for them, and re-layouts: none -> 4.79 us  [product(): out = outs[0] if len(outs) == 1 else jnp.concatenate(outs, axis=1)]
    ppermute x8 -> x7, waiting for transfers between devices: 36.8 us -> 40.2 us  [shift_axis(): lax.ppermute(cells, axis, [(i, (i + offset) % count) for i in range(count)])]
  transfers between devices with their start and end apart: 21 -> 17, of which waited for: 5 -> 8; matrix products, arithmetic and copies ran while one was open for 30% -> 20% of each run, Pallas kernels for 0% -> 0%
where the time goes in v3:
time: 265 us; the launch traced here: 264 us
  waiting for transfers between devices  72.3 us (27%)
  blocking collectives  62 us (23%)
  matrix products  57.8 us (22%)
  other arithmetic  31.7 us (12%)
  local copies, waits for them, and re-layouts  19.6 us (7%)
  starting transfers between devices  17.4 us (7%)
  between operations  3.15 us (1%)
    psum x1, blocking collectives, body(): lax.psum(sum((jnp.sum(r * r) for r in raw)), ('sec', 'seq', 'trk'))  40.6 us
    ppermute x7, waiting for transfers between devices, shift_axis(): lax.ppermute(cells, axis, [(i, (i + offset) % count) for i in range(count)])  40.2 us
    ppermute x4, waiting for transfers between devices, shift_seq(): lax.ppermute(cells, 'seq', [(i, (i + offset * CORES) % count) for i in ra...  32 us
    all_gather x1, blocking collectives, body(): gathered = lax.all_gather(mixed_share, 'trk', axis=0)  21.4 us
    dot_general x10, matrix products, product(): lax.dot_general(left[:, k * inner * size:(k + 1) * inner * size], right,...  15.1 us
    dot_general x1, matrix products, body(): logits = jnp.dot(mixed, weights, preferred_element_type=jnp.float32)  13.9 us
    dot_general x4, matrix products, picked(): jnp.dot(cells, choice.astype(cells.dtype), preferred_element_type=jnp.flo...  11.6 us
    dot_general x1, matrix products, body(): lax.dot_general(delta, weights, (((1,), (1,)), ((), ())), preferred_eleme...  10.9 us
  transfers between devices with their start and end apart: 17, of which 8 were waited for; matrix products, arithmetic and copies ran while one was open for 20% of the time, Pallas kernels for 0%

profile of v3, /device:TPU:0, one launch (start us, length us, event | category | flops | bytes accessed | tf_op | source)
XLA Modules:
  0.0 264.0 jit_solution(10085287895439506711)
XLA Ops:
  6.8 3.8 %collective-permute-start = (bf16[4,16,1536]{2,1,0:T(8,128)(2,1)}, bf16[4,16,1536]{2,1,0:T(8,128)(2,1)}, u32[]{:S(2)}, u32[]{:S(2)}) collective-permute-start(bf16[4,16,1536]{2,1,0:T(8,128)(2,1)} %get-tuple-element.19), channel_id=1, source_target_pairs={{0,4},{4,8},{8,12},{1,5},{5,9},{9,13},{2,6},{6,10},{10,14},{3,7},{... | collective-permute-start | bytes 589832 | tf_op jit(solution)/shard_map/ppermute | solution.py:24
  11.1 2.6 fusion.45
  13.7 3.0 %convert.14 = f32[32,8,40,128]{3,2,1,0:T(8,128)} convert(bf16[32,8,40,128]{3,2,1,0:T(8,128)(2,1)S(1)} %bitcast.146) | non-fusion elementwise | flops 1310720 | bytes 7864320
  22.7 21.4 %all-gather = bf16[1024,384]{1,0:T(8,128)(2,1)S(1)} all-gather(bf16[256,384]{1,0:T(8,128)(2,1)S(1)} %fusion.51), channel_id=2, replica_groups=mesh['sec'=2,'seq'=4,'trk'=4] {'trk'}, dimensions={0}, use_global_device_ids=true | all-gather | bytes 983040 | tf_op jit(solution)/shard_map/all_gather | solution.py:150
  45.1 13.9 %fusion.8 = bf16[256,5120]{1,0:T(8,128)(2,1)S(1)} fusion(f32[32,8,40,128]{3,2,1,0:T(8,128)} %convert.14, f32[4,5120]{1,0:T(4,128)S(1)} %fusion.80, bf16[192,8,40,128]{3,2,1,0:T(8,128)(2,1)} %bitcast.140, bf16[256,384]{1,0:T(8,128)(2,1)S(1)} %get-tuple-element.16, bf16[256,384]{1,0:T(8,128)(2,1)S(1)} %get-tuple-element.14, ...), kind=kOutput, calls=%fused_computation.9 | convolution fusion | flops 4045406208 | bytes 24461312 | tf_op jit(solution)/shard_map/dot_general | solution.py:158
  59.1 10.9 %fusion = f32[256,1536]{1,0:T(8,128)} fusion(bf16[256,5120]{1,0:T(8,128)(2,1)S(1)} %fusion.8, bf16[192,8,40,128]{3,2,1,0:T(8,128)(2,1)} %bitcast.141), kind=kOutput, calls=%fused_computation | convolution fusion | flops 4026531840 | bytes 19922944 | tf_op jit(solution)/shard_map/dot_general | solution.py:166
  75.9 4.3 %collective-permute-done.5 = bf16[256,384]{1,0:T(8,128)(2,1)S(1)} collective-permute-done((bf16[256,384]{1,0:T(8,128)(2,1)S(1)}, bf16[256,384]{1,0:T(8,128)(2,1)S(1)}, u32[]{:S(2)}, u32[]{:S(2)}) %collective-permute-start.5) | collective-permute-done | bytes 196640 | tf_op jit(solution)/shard_map/ppermute | solution.py:52
  80.2 10.8 %collective-permute-done.4 = bf16[256,384]{1,0:T(8,128)(2,1)S(1)} collective-permute-done((bf16[256,384]{1,0:T(8,128)(2,1)S(1)}, bf16[256,384]{1,0:T(8,128)(2,1)S(1)}, u32[]{:S(2)}, u32[]{:S(2)}) %collective-permute-start.4) | collective-permute-done | bytes 196640 | tf_op jit(solution)/shard_map/ppermute | solution.py:52
  96.0 3.5 %fusion.34 = bf16[8,96,768]{2,1,0:T(8,128)(2,1)S(1)} fusion(s32[768]{0:T(1024)S(1)} %get-tuple-element.25, bf16[4,96,1536]{2,1,0:T(8,128)(2,1)S(1)} %collective-permute-done.2, bf16[4,16,1536]{2,1,0:T(8,128)(2,1)} %collective-permute-done.1, bf16[4,64,1536]{2,1,0:T(8,128)(2,1)S(1)} %fusion.28, bf16[4,16,1536]{2,1,0:T(8,128)(2,1)} %collective-permute-done), kind=kOutput, calls=%fused_computation.54 | convolution fusion | flops 1823145984 | bytes 3542016 | tf_op jit(solution)/shard_map/dot_general | solution.py:78
  102.1 2.7 %copy.11 = f32[384,768]{1,0:T(8,128)} copy(f32[384,768]{0,1:T(8,128)} %pad_maximum_fusion.5) | data formatting | bytes 2359296 | tf_op jit(solution)/shard_map/concatenate | solution.py:102
  112.3 3.4 %fusion.15 = bf16[8,96,768]{2,1,0:T(8,128)(2,1)S(1)} fusion(s32[768]{0:T(1024)S(1)} %get-tuple-element.26, bf16[4,96,1536]{2,1,0:T(8,128)(2,1)} %copy-done.16, bf16[4,16,1536]{2,1,0:T(8,128)(2,1)} %collective-permute-done.1, bf16[4,64,1536]{2,1,0:T(8,128)(2,1)S(1)} %fusion.28, bf16[4,16,1536]{2,1,0:T(8,128)(2,1)} %collective-permute-done), kind=kOutput, calls=%fused_computation.19 | convolution fusion | flops 1822556160 | bytes 3542016 | tf_op jit(solution)/shard_map/dot_general | solution.py:78
  121.4 4.0 %collective-permute-done.9 = bf16[2,192,384]{2,1,0:T(8,128)(2,1)S(1)} collective-permute-done((bf16[2,192,384]{2,1,0:T(8,128)(2,1)S(1)}, bf16[2,192,384]{2,1,0:T(8,128)(2,1)S(1)}, u32[]{:S(2)}, u32[]{:S(2)}) %collective-permute-start.9) | collective-permute-done | bytes 294944 | tf_op jit(solution)/shard_map/ppermute | solution.py:52
  130.7 2.8 %convolution_convert_fusion = bf16[384,2560]{1,0:T(8,128)(2,1)S(1)} fusion(bf16[512,768]{1,0:T(8,128)(2,1)S(1)} %copy-done.9, bf16[256,5120]{1,0:T(8,128)(2,1)} %collective-permute-done.12, bf16[256,5120]{1,0:T(8,128)(2,1)S(1)} %fusion.8), kind=kOutput, calls=%fused_computation.20 | convolution fusion | flops 1012858880 | bytes 7602176 | tf_op jit(solution)/shard_map/dot_general | solution.py:94
  134.0 2.5 fusion.57
  136.6 2.5 fusion.60
  139.1 30.2 %collective-permute-done.13 = bf16[2,192,2560]{2,1,0:T(8,128)(2,1)S(1)} collective-permute-done((bf16[2,192,2560]{2,1,0:T(8,128)(2,1)S(1)}, bf16[2,192,2560]{2,1,0:T(8,128)(2,1)S(1)}, u32[]{:S(2)}, u32[]{:S(2)}) %collective-permute-start.13) | collective-permute-done | bytes 1966112 | tf_op jit(solution)/shard_map/ppermute | solution.py:45
  172.6 8.9 %collective-permute-done.15 = bf16[2,192,2560]{2,1,0:T(8,128)(2,1)S(1)} collective-permute-done((bf16[2,192,2560]{2,1,0:T(8,128)(2,1)S(1)}, bf16[2,192,2560]{2,1,0:T(8,128)(2,1)S(1)}, u32[]{:S(2)}, u32[]{:S(2)}) %collective-permute-start.15) | collective-permute-done | bytes 1966112 | tf_op jit(solution)/shard_map/ppermute | solution.py:52
  188.5 12.3 %collective-permute-done.14 = bf16[192,2560]{1,0:T(8,128)(2,1)S(1)} collective-permute-done((bf16[192,2560]{1,0:T(8,128)(2,1)}, bf16[192,2560]{1,0:T(8,128)(2,1)S(1)}, u32[]{:S(2)}, u32[]{:S(2)}) %collective-permute-start.14) | collective-permute-done | bytes 983072 | tf_op jit(solution)/shard_map/ppermute | solution.py:52
  200.8 2.7 %multiply_reduce_fusion.1 = f32[]{:T(128)} fusion(bf16[192,2560]{1,0:T(8,128)(2,1)S(1)} %collective-permute-done.14, f32[2,192,2560]{2,1,0:T(8,128)} %copy-done, s32[]{:T(128)S(6)} %select_n.186), kind=kLoop, calls=%fused_computation.37 | loop fusion | flops 1966079 | bytes 2949128 | tf_op jit(solution)/shard_map/reduce_sum | solution.py:210
  208.2 40.6 %psum.7 = f32[]{:T(128)} all-reduce(f32[]{:T(128)S(6)} %add.373), channel_id=1, replica_groups=mesh['sec'=2,'seq'=4,'trk'=4] {'sec','seq','trk'}, use_global_device_ids=true, to_apply=%region_3.4 | all-reduce | flops 1 | bytes 8 | tf_op jit(solution)/shard_map/psum | solution.py:210
  249.5 3.1 %fusion.40 = f32[192,2560]{1,0:T(8,128)} fusion(bf16[192,2560]{1,0:T(8,128)(2,1)S(1)} %collective-permute-done.16, f32[2,192,2560]{2,1,0:T(8,128)} %copy-done.1, s32[]{:T(128)S(6)} %select_n.189, f32[]{:T(128)S(6)} %min.3), kind=kLoop, calls=%fused_computation.58 | loop fusion | flops 1474560 | bytes 4915208 | tf_op jit(solution)/shard_map/mul | solution.py:214
  254.2 3.1 %fusion.39 = f32[192,2560]{1,0:T(8,128)} fusion(bf16[192,2560]{1,0:T(8,128)(2,1)S(1)} %collective-permute-done.14, f32[2,192,2560]{2,1,0:T(8,128)} %copy-done, s32[]{:T(128)S(6)} %select_n.186, f32[]{:T(128)S(6)} %min.3), kind=kLoop, calls=%fused_computation.57 | loop fusion | flops 1474560 | bytes 4915208 | tf_op jit(solution)/shard_map/mul | solution.py:214
  257.3 2.8 %reshape.288 = f32[192,1,20,128]{3,2,0,1:T(8,128)} reshape(f32[192,2560]{1,0:T(8,128)} %fusion.39) | data formatting | bytes 3932160 | tf_op jit(solution)/shard_map/reshape | solution.py:214
  260.1 4.0 %maximum_bitcast_fusion = f32[192,1,40,128]{3,2,1,0:T(8,128)} fusion(f32[192,1,20,128]{3,2,0,1:T(8,128)S(1)} %reshape.289, f32[192,1,20,128]{3,2,0,1:T(8,128)} %reshape.288), kind=kLoop, calls=%fused_computation.22 | loop fusion | flops 983040 | bytes 7864320
  (126 shorter events, 61.3 us)
Async XLA Ops:
  0.6 9.9 %copy-start.19 = (s32[1,40]{1,0:T(1,128)S(1)}, s32[1,40]{1,0:T(1,128)}, u32[]{:S(2)}) copy-start(s32[1,40]{1,0:T(1,128)} %param.12) | copy-start | bytes 484
  0.6 10.0 %copy-start.20 = (s32[4]{0:T(128)S(1)}, s32[4]{0:T(128)}, u32[]{:S(2)}) copy-start(s32[4]{0:T(128)} %param.13) | copy-start | bytes 52
  2.7 11.0 %copy-start.6 = (bf16[4,64,1,40,128]{4,3,2,1,0:T(8,128)(2,1)S(1)}, bf16[4,64,1,40,128]{4,3,2,1,0:T(8,128)(2,1)}, u32[]{:S(2)}) copy-start(bf16[4,64,1,40,128]{4,3,2,1,0:T(8,128)(2,1)} %param.11) | copy-start | bytes 7864324
  5.5 12.1 %collective-permute-start.1 = (bf16[4,16,1536]{2,1,0:T(8,128)(2,1)}, bf16[4,16,1536]{2,1,0:T(8,128)(2,1)}, u32[]{:S(2)}, u32[]{:S(2)}) collective-permute-start(bf16[4,16,1536]{2,1,0:T(8,128)(2,1)} %get-tuple-element.20), channel_id=1, source_target_pairs={{4,0},{8,4},{12,8},{5,1},{9,5},{13,9},{6,2},{10,6},{14,10},{7,3},{... | collective-permute-start | bytes 589832 | tf_op jit(solution)/shard_map/ppermute | solution.py:26
  6.8 10.9 %collective-permute-start = (bf16[4,16,1536]{2,1,0:T(8,128)(2,1)}, bf16[4,16,1536]{2,1,0:T(8,128)(2,1)}, u32[]{:S(2)}, u32[]{:S(2)}) collective-permute-start(bf16[4,16,1536]{2,1,0:T(8,128)(2,1)} %get-tuple-element.19), channel_id=1, source_target_pairs={{0,4},{4,8},{8,12},{1,5},{5,9},{9,13},{2,6},{6,10},{10,14},{3,7},{... | collective-permute-start | bytes 589832 | tf_op jit(solution)/shard_map/ppermute | solution.py:24
  71.5 19.7 %collective-permute-start.11 = (bf16[256,1536]{1,0:T(8,128)(2,1)S(1)}, bf16[256,1536]{1,0:T(8,128)(2,1)S(1)}, u32[]{:S(2)}, u32[]{:S(2)}) collective-permute-start(bf16[256,1536]{1,0:T(8,128)(2,1)S(1)} %copy-done.10), channel_id=1, source_target_pairs={{0,4},{4,0},{8,12},{12,8},{1,5},{5,1},{9,13},{13,9},{2,6},{6,2},{1... | collective-permute-start | bytes 2359304 | tf_op jit(solution)/shard_map/ppermute | solution.py:56
  71.8 8.4 %collective-permute-start.5 = (bf16[256,384]{1,0:T(8,128)(2,1)S(1)}, bf16[256,384]{1,0:T(8,128)(2,1)S(1)}, u32[]{:S(2)}, u32[]{:S(2)}) collective-permute-start(bf16[256,384]{1,0:T(8,128)(2,1)S(1)} %get-tuple-element.5), channel_id=1, source_target_pairs={{0,3},{1,0},{2,1},{3,2},{4,7},{5,4},{6,5},{7,6},{8,11},{9,8},{10,9... | collective-permute-start | bytes 589832 | tf_op jit(solution)/shard_map/ppermute | solution.py:52
  73.7 17.3 %collective-permute-start.4 = (bf16[256,384]{1,0:T(8,128)(2,1)S(1)}, bf16[256,384]{1,0:T(8,128)(2,1)S(1)}, u32[]{:S(2)}, u32[]{:S(2)}) collective-permute-start(bf16[256,384]{1,0:T(8,128)(2,1)S(1)} %get-tuple-element.6), channel_id=1, source_target_pairs={{0,2},{1,3},{2,0},{3,1},{4,6},{5,7},{6,4},{7,5},{8,10},{9,11},{10,... | collective-permute-start | bytes 589832 | tf_op jit(solution)/shard_map/ppermute | solution.py:52
  73.7 17.3 %collective-permute-start.3 = (bf16[256,384]{1,0:T(8,128)(2,1)S(1)}, bf16[256,384]{1,0:T(8,128)(2,1)S(1)}, u32[]{:S(2)}, u32[]{:S(2)}) collective-permute-start(bf16[256,384]{1,0:T(8,128)(2,1)S(1)} %get-tuple-element.4), channel_id=1, source_target_pairs={{0,1},{1,2},{2,3},{3,0},{4,5},{5,6},{6,7},{7,4},{8,9},{9,10},{10,1... | collective-permute-start | bytes 589832 | tf_op jit(solution)/shard_map/ppermute | solution.py:52
  75.8 20.2 %collective-permute-start.2 = (bf16[4,96,1536]{2,1,0:T(8,128)(2,1)S(1)}, bf16[4,96,1536]{2,1,0:T(8,128)(2,1)S(1)}, u32[]{:S(2)}, u32[]{:S(2)}) collective-permute-start(bf16[4,96,1536]{2,1,0:T(8,128)(2,1)S(1)} %pad_maximum_fusion.4), channel_id=1, source_target_pairs={{0,4},{4,0},{8,12},{12,8},{1,5},{5,1},{9,13},{13,9},{2,6},{6,2},{1... | collective-permute-start | bytes 3538952 | tf_op jit(solution)/shard_map/ppermute | solution.py:56
  80.2 37.5 %collective-permute-start.12 = (bf16[256,5120]{1,0:T(8,128)(2,1)S(1)}, bf16[256,5120]{1,0:T(8,128)(2,1)}, u32[]{:S(2)}, u32[]{:S(2)}) collective-permute-start(bf16[256,5120]{1,0:T(8,128)(2,1)S(1)} %fusion.8), channel_id=1, source_target_pairs={{0,4},{4,0},{8,12},{12,8},{1,5},{5,1},{9,13},{13,9},{2,6},{6,2},{1... | collective-permute-start | bytes 7864328 | tf_op jit(solution)/shard_map/ppermute | solution.py:56
  91.1 9.0 %copy-start.14 = (bf16[256,384]{1,0:T(8,128)(2,1)}, bf16[256,384]{1,0:T(8,128)(2,1)S(1)}, u32[]{:S(2)}) copy-start(bf16[256,384]{1,0:T(8,128)(2,1)S(1)} %fusion.73) | copy-start | bytes 589828
  91.1 8.5 %collective-permute-start.6 = (bf16[256,384]{1,0:T(8,128)(2,1)S(1)}, bf16[256,384]{1,0:T(8,128)(2,1)S(1)}, u32[]{:S(2)}, u32[]{:S(2)}) collective-permute-start(bf16[256,384]{1,0:T(8,128)(2,1)S(1)} %fusion.73), channel_id=1, source_target_pairs={{0,4},{4,0},{8,12},{12,8},{1,5},{5,1},{9,13},{13,9},{2,6},{6,2},{1... | collective-permute-start | bytes 589832 | tf_op jit(solution)/shard_map/ppermute | solution.py:56
  110.9 16.3 %collective-permute-start.7 = (bf16[2,192,768]{2,1,0:T(8,128)(2,1)}, bf16[2,192,768]{2,1,0:T(8,128)(2,1)S(1)}, u32[]{:S(2)}, u32[]{:S(2)}) collective-permute-start(bf16[2,192,768]{2,1,0:T(8,128)(2,1)} %bitcast.156), channel_id=1, source_target_pairs={{0,8},{4,12},{8,0},{12,4},{1,9},{5,13},{9,1},{13,5},{2,10},{6,14},... | collective-permute-start | bytes 1769480 | tf_op jit(solution)/shard_map/ppermute | solution.py:45
  116.2 9.2 %collective-permute-start.9 = (bf16[2,192,384]{2,1,0:T(8,128)(2,1)S(1)}, bf16[2,192,384]{2,1,0:T(8,128)(2,1)S(1)}, u32[]{:S(2)}, u32[]{:S(2)}) collective-permute-start(bf16[2,192,384]{2,1,0:T(8,128)(2,1)S(1)} %bitcast.161), channel_id=1, source_target_pairs={{0,16},{16,0},{1,17},{17,1},{2,18},{18,2},{3,19},{19,3},{4,20},{20... | collective-permute-start | bytes 884744 | tf_op jit(solution)/shard_map/ppermute | solution.py:52
  120.3 49.1 %collective-permute-start.13 = (bf16[2,192,2560]{2,1,0:T(8,128)(2,1)S(1)}, bf16[2,192,2560]{2,1,0:T(8,128)(2,1)S(1)}, u32[]{:S(2)}, u32[]{:S(2)}) collective-permute-start(bf16[2,192,2560]{2,1,0:T(8,128)(2,1)S(1)} %bitcast.160), channel_id=1, source_target_pairs={{0,8},{4,12},{8,0},{12,4},{1,9},{5,13},{9,1},{13,5},{2,10},{6,14},... | collective-permute-start | bytes 5898248 | tf_op jit(solution)/shard_map/ppermute | solution.py:45
  126.1 59.5 %collective-permute-start.10 = (bf16[192,384]{1,0:T(8,128)(2,1)}, bf16[192,384]{1,0:T(8,128)(2,1)S(1)}, u32[]{:S(2)}, u32[]{:S(2)}) collective-permute-start(bf16[192,384]{1,0:T(8,128)(2,1)} %fusion.79), channel_id=1, source_target_pairs={{0,8},{4,12},{8,0},{12,4},{1,9},{5,13},{9,1},{13,5},{2,10},{6,14},... | collective-permute-start | bytes 442376 | tf_op jit(solution)/shard_map/ppermute | solution.py:45
  129.1 58.3 %collective-permute-start.8 = (bf16[192,768]{1,0:T(8,128)(2,1)}, bf16[192,768]{1,0:T(8,128)(2,1)}, u32[]{:S(2)}, u32[]{:S(2)}) collective-permute-start(bf16[192,768]{1,0:T(8,128)(2,1)} %fusion.74), channel_id=1, source_target_pairs={{0,16},{16,0},{1,17},{17,1},{2,18},{18,2},{3,19},{19,3},{4,20},{20... | collective-permute-start | bytes 884744 | tf_op jit(solution)/shard_map/ppermute | solution.py:52
  133.5 48.0 %collective-permute-start.15 = (bf16[2,192,2560]{2,1,0:T(8,128)(2,1)S(1)}, bf16[2,192,2560]{2,1,0:T(8,128)(2,1)S(1)}, u32[]{:S(2)}, u32[]{:S(2)}) collective-permute-start(bf16[2,192,2560]{2,1,0:T(8,128)(2,1)S(1)} %bitcast.147), channel_id=1, source_target_pairs={{0,16},{16,0},{1,17},{17,1},{2,18},{18,2},{3,19},{19,3},{4,20},{20... | collective-permute-start | bytes 5898248 | tf_op jit(solution)/shard_map/ppermute | solution.py:52
  169.9 12.1 %copy-start = (f32[2,192,2560]{2,1,0:T(8,128)}, f32[2,192,2560]{2,1,0:T(8,128)S(1)}, u32[]{:S(2)}) copy-start(f32[2,192,2560]{2,1,0:T(8,128)S(1)} %convert_add_fusion.1) | copy-start | bytes 11796484
  171.1 29.7 %collective-permute-start.14 = (bf16[192,2560]{1,0:T(8,128)(2,1)}, bf16[192,2560]{1,0:T(8,128)(2,1)S(1)}, u32[]{:S(2)}, u32[]{:S(2)}) collective-permute-start(bf16[192,2560]{1,0:T(8,128)(2,1)} %fusion.54), channel_id=1, source_target_pairs={{0,16},{16,0},{1,17},{17,1},{2,18},{18,2},{3,19},{19,3},{4,20},{20... | collective-permute-start | bytes 2949128 | tf_op jit(solution)/shard_map/ppermute | solution.py:52
  184.2 20.5 %collective-permute-start.16 = (bf16[192,2560]{1,0:T(8,128)(2,1)}, bf16[192,2560]{1,0:T(8,128)(2,1)S(1)}, u32[]{:S(2)}, u32[]{:S(2)}) collective-permute-start(bf16[192,2560]{1,0:T(8,128)(2,1)} %fusion.55), channel_id=1, source_target_pairs={{0,8},{4,12},{8,0},{12,4},{1,9},{5,13},{9,1},{13,5},{2,10},{6,14},... | collective-permute-start | bytes 2949128 | tf_op jit(solution)/shard_map/ppermute | solution.py:45
  188.4 16.3 %copy-start.2 = (f32[2,192,2560]{2,1,0:T(8,128)S(1)}, f32[2,192,2560]{2,1,0:T(8,128)}, u32[]{:S(2)}) copy-start(f32[2,192,2560]{2,1,0:T(8,128)} %copy-done.1) | copy-start | bytes 11796484
  188.5 18.7 %copy-start.8 = (f32[192,1,384]{2,0,1:T(8,128)S(1)}, f32[192,1,384]{2,0,1:T(8,128)}, u32[]{:S(2)}) copy-start(f32[192,1,384]{2,0,1:T(8,128)} %fusion.75) | copy-start | bytes 884740
  (15 other events, 46.4 us)
